TPU v7x, 256 devices: a whole 4x4x8 slice. The times are simulated.
256 devices in a mesh: view: 8 (over x, core), gs: 32 (over z, y).
Axes of the slice: x: 4, y: 4, z: 8, core: 2. Of those that a mesh axis runs over, the one named last changes fastest.
Arguments:
- params: float32 [59, 262144], P(None, 'gs'), as said below
- cam_pos: float32 [8, 3], P('view'), may hold values from -0.03 to 0.03
- req_ids: int32 [8, 32, 32, 64], P('view', 'gs'), may hold values from 0 to 8191, as said below
- tile_slots: int32 [8, 512, 64], P('view', 'gs'), may hold values from 0 to 2047, as said below
- tile_len: int32 [8, 512], P('view', 'gs'), may hold values from 1 to 64, as said below
- cotangent: float32 [8, 3, 131072], P('view', None, 'gs'), may hold values from -6 to 6
Outputs:
- rendered: float32 [8, 3, 131072], P('view', None, 'gs')
- grads: float32 [59, 262144], P(None, ('gs', 'view'))
Inputs may be any that keep to these rules, and one draw needn't show every extreme that they name: `req_ids`: within each view, renderer and owner the 64 ids are distinct, and within a view two renderers never ask an owner for the same id. `tile_slots`: the 64 slots of a tile's list are distinct, and within a view no slot stands in two lists of the same renderer. `tile_len`: the first tile of every renderer has all 64 entries live. `params`: row 0 within [-3.4, 3.4], row 1 within [-3.4 h, 3.4 h] with h = 2, row 2 within [2, 4], rows 3 to 5 within [log 0.02, log 0.12], row 6 within [1, 2], rows 7 to 9 within [-1, 1], row 10 within [-4.5, 1].
All inputs are finite; a program needn't handle non-finite values.
Results may differ from a plain program's by a relative error of at most 0.0003.
Values sent between devices are 32-bit elements; how exact they have to be, the bound alone decides.
A program may use at most 64 MiB of HBM per device.

v0:
```python
import functools

import jax
import jax.numpy as jnp
from jax import lax
from jax.experimental import pallas as pl
from jax.experimental.pallas import tpu as pltpu
from jax.sharding import PartitionSpec as P

MESH = pl.DeviceIdType.MESH
F32 = jnp.float32
BF16 = jnp.bfloat16
TILES = 16
ENTRIES = 64
ROWS = TILES * ENTRIES
PIXELS = 256
CAP = 64
LANES = 128

focal = 1.2 * 128.0
dilate = 0.3
sh_zero = 0.28209479177387814
sh_one = 0.4886025119029199
sh_two = [
    1.0925484305920792,
    -1.0925484305920792,
    0.31539156525252005,
    -1.0925484305920792,
    0.5462742152960396,
]
sh_three = [
    -0.5900435899266435,
    2.890611442640554,
    -0.4570457994644658,
    0.3731763325901154,
    -0.4570457994644658,
    1.445305721320277,
    -0.5900435899266435,
]


def covariance(log_scales, quat):
    squares = [jnp.exp(2.0 * value) for value in log_scales]
    norm_sq = quat[0] * quat[0] + quat[1] * quat[1] + quat[2] * quat[2] + quat[3] * quat[3]
    inv_norm = 1.0 / jnp.sqrt(norm_sq)
    w, x, y, z = [value * inv_norm for value in quat]
    rotation = [
        [1 - 2 * (y * y + z * z), 2 * (x * y - w * z), 2 * (x * z + w * y)],
        [2 * (x * y + w * z), 1 - 2 * (x * x + z * z), 2 * (y * z - w * x)],
        [2 * (x * z - w * y), 2 * (y * z + w * x), 1 - 2 * (x * x + y * y)],
    ]
    scaled = [[rotation[i][j] * squares[j] for j in range(3)] for i in range(3)]

    def entry(i, j):
        return (
            scaled[i][0] * rotation[j][0]
            + scaled[i][1] * rotation[j][1]
            + scaled[i][2] * rotation[j][2]
        )

    return [entry(0, 0), entry(0, 1), entry(0, 2), entry(1, 1), entry(1, 2), entry(2, 2)]


def geometry(x, y, z, sigma):
    s00, s01, s02, s11, s12, s22 = sigma
    inv_z = 1.0 / z
    jac = focal * inv_z
    center_x = jac * x
    center_y = jac * y
    jac_x = -center_x * inv_z
    jac_y = -center_y * inv_z
    jac_sq = jac * jac
    cov_a = jac_sq * s00 + 2.0 * (jac * jac_x) * s02 + jac_x * jac_x * s22 + dilate
    cov_b = jac_sq * s01 + jac * (jac_y * s02 + jac_x * s12) + jac_x * jac_y * s22
    cov_c = jac_sq * s11 + 2.0 * (jac * jac_y) * s12 + jac_y * jac_y * s22 + dilate
    inv_det = 1.0 / (cov_a * cov_c - cov_b * cov_b)
    return center_x, center_y, cov_c * inv_det, -cov_b * inv_det, cov_a * inv_det


def harmonic_basis(x, y, z):
    inv_distance = 1.0 / jnp.sqrt(x * x + y * y + z * z)
    dx = x * inv_distance
    dy = y * inv_distance
    dz = z * inv_distance
    xx = dx * dx
    yy = dy * dy
    zz = dz * dz
    xy = dx * dy
    yz = dy * dz
    xz = dx * dz
    return [
        -sh_one * dy,
        sh_one * dz,
        -sh_one * dx,
        sh_two[0] * xy,
        sh_two[1] * yz,
        sh_two[2] * (2 * zz - xx - yy),
        sh_two[3] * xz,
        sh_two[4] * (xx - yy),
        sh_three[0] * dy * (3 * xx - yy),
        sh_three[1] * xy * dz,
        sh_three[2] * dy * (4 * zz - xx - yy),
        sh_three[3] * dz * (2 * zz - 3 * xx - 3 * yy),
        sh_three[4] * dx * (4 * zz - xx - yy),
        sh_three[5] * dz * (xx - yy),
        sh_three[6] * dx * (xx - 3 * yy),
    ]


def pieces(value, count):
    out = []
    for at in range(count):
        piece = value.astype(BF16)
        out.append(piece)
        if at + 1 < count:
            value = value - piece.astype(F32)
    return out


def dot(left, right, dims):
    return lax.dot_general(left, right, ((dims[0], dims[1]), ((), ())), preferred_element_type=F32)


def iota(shape, axis):
    return lax.broadcasted_iota(jnp.int32, shape, axis)


def kernel(
    owners,
    views,
    params_ref,
    cam_ref,
    ids_ref,
    slots_ref,
    len_ref,
    cot_ref,
    image_ref,
    grads_ref,
    held,
    held_cot,
    image,
    summed,
    ids_out,
    ids_in,
    cam_out,
    cam_in,
    table,
    low_hot,
    high_hot,
    feat_out,
    feat_in,
    wide,
    exponent,
    along,
    alpha_all,
    blend_all,
    split_a,
    split_b,
    split_c,
    split_d,
    grad_out,
    grad_in,
    dense,
    view_in,
    load_sem,
    store_sem,
    ids_s,
    ids_r,
    feat_s,
    feat_r,
    grad_s,
    grad_r,
    cam_s,
    cam_r,
    view_s,
    view_r,
):
    me = lax.axis_index("gs")
    my_view = lax.axis_index("view")
    blocks = held.shape[1]
    chunk = blocks // views
    slots_all = owners * CAP
    slot_tiles = slots_all // LANES

    def load(j):
        return pltpu.make_async_copy(
            params_ref.at[:, pl.ds(pl.multiple_of(j * LANES, LANES), LANES)],
            held.at[:, j, :],
            load_sem.at[0],
        )

    def load_body(j, carry):
        load(j).start()
        return carry

    lax.fori_loop(0, blocks, load_body, 0)

    pltpu.make_async_copy(cot_ref, held_cot, load_sem.at[1]).start()

    barrier = pltpu.get_barrier_semaphore()

    def greet(off, carry):
        peer = lax.rem(me + off, owners)
        pl.semaphore_signal(barrier, inc=1, device_id=(my_view, peer), device_id_type=MESH)
        return carry

    lax.fori_loop(1, owners, greet, 0)

    def greet_view(off, carry):
        peer = lax.rem(my_view + off, views)
        pl.semaphore_signal(barrier, inc=1, device_id=(peer, me), device_id_type=MESH)
        return carry

    lax.fori_loop(1, views, greet_view, 0)

    def gs_copy(out, into, send, recv, to, sender):
        return pltpu.make_async_remote_copy(
            src_ref=out.at[to],
            dst_ref=into.at[sender],
            send_sem=send.at[to],
            recv_sem=recv.at[sender],
            device_id=(my_view, to),
            device_id_type=MESH,
        )

    def gs_send(out, into, send, recv):
        def body(off, carry):
            peer = lax.rem(me + off, owners)
            gs_copy(out, into, send, recv, peer, me).start()
            return carry

        lax.fori_loop(1, owners, body, 0)

    def gs_wait_recv(out, into, send, recv):
        def body(off, carry):
            peer = lax.rem(me + off, owners)
            gs_copy(out, into, send, recv, peer, peer).wait_recv()
            return carry

        lax.fori_loop(1, owners, body, 0)

    def gs_wait_send(out, into, send, recv):
        def body(off, carry):
            peer = lax.rem(me + off, owners)
            gs_copy(out, into, send, recv, peer, me).wait_send()
            return carry

        lax.fori_loop(1, owners, body, 0)

    asked = ids_ref[...]
    doubled = jnp.concatenate([asked, asked], axis=1)
    my_half = (iota(doubled.shape, 1) >> 6) == lax.rem(me, 2)
    ids_out[...] = jnp.where(my_half, doubled, 0).reshape(owners, 1, LANES)
    cam_x = cam_ref[0, 0]
    cam_y = cam_ref[0, 1]
    cam_z = cam_ref[0, 2]
    cam_row = iota((8, LANES), 0)
    cam_tile = jnp.where(cam_row == 0, cam_x, jnp.where(cam_row == 1, cam_y, cam_z))
    cam_out[...] = cam_tile

    pl.semaphore_wait(barrier, owners + views - 2)

    gs_send(ids_out, ids_in, ids_s, ids_r)
    ids_in[me] = ids_out[me]

    def cam_copy(to, sender):
        return pltpu.make_async_remote_copy(
            src_ref=cam_out,
            dst_ref=cam_in.at[sender],
            send_sem=cam_s.at[to],
            recv_sem=cam_r.at[sender],
            device_id=(to, me),
            device_id_type=MESH,
        )

    def cam_send(off, carry):
        cam_copy(lax.rem(my_view + off, views), my_view).start()
        return carry

    lax.fori_loop(1, views, cam_send, 0)
    cam_in[my_view] = cam_tile

    pltpu.make_async_copy(held, held, load_sem.at[0]).wait()

    def features_body(at, carry):
        rows = pl.ds(pl.multiple_of(at * 16, 16), 16)

        def get(r):
            return held[r, rows, :]

        x = get(0) - cam_x
        y = get(1) - cam_y
        z = get(2) - cam_z
        sigma = covariance([get(3), get(4), get(5)], [get(6), get(7), get(8), get(9)])
        values = list(geometry(x, y, z, sigma))
        values.append(-jnp.log(1.0 + jnp.exp(-get(10))))
        basis = harmonic_basis(x, y, z)
        for c in range(3):
            total = sh_zero * get(11 + 16 * c) + 0.5
            for k in range(15):
                total = total + basis[k] * get(12 + 16 * c + k)
            values.append(total)
        half = lax.div(at, 2)
        inner = lax.rem(at, 2)
        lanes = pl.ds(pl.multiple_of(half * LANES, LANES), LANES)
        for c in range(9):
            for s, piece in enumerate(pieces(values[c], 3)):
                table[s, pl.ds(pl.multiple_of(c * 32 + inner * 16, 16), 16), lanes] = piece
        return carry

    lax.fori_loop(0, blocks // 16, features_body, 0)

    gs_wait_recv(ids_out, ids_in, ids_s, ids_r)

    def hot_body(at, carry):
        ids = ids_in[2 * at] + ids_in[2 * at + 1]
        low = (ids & (LANES - 1)) + ((ids >> 12) << 7)
        high = (ids >> 7) & 31
        lanes = pl.ds(pl.multiple_of(at * LANES, LANES), LANES)
        low_hot[:, lanes] = (iota((256, LANES), 0) == low).astype(F32).astype(BF16)
        high_hot[:, lanes] = (iota((32, LANES), 0) == high).astype(F32)
        return carry

    lax.fori_loop(0, slot_tiles, hot_body, 0)

    lane_half = iota((8, LANES), 1) < CAP

    def gather_body(at, carry):
        lanes = pl.ds(pl.multiple_of(at * 256, 256), 256)
        right = low_hot[:, lanes]
        picked = dot(table[0], right, ((1,), (0,)))
        picked += dot(table[1], right, ((1,), (0,)))
        picked += dot(table[2], right, ((1,), (0,)))
        mask = high_hot[:, lanes]
        rows = [
            jnp.sum(picked[c * 32 : c * 32 + 32] * mask, axis=0, keepdims=True) for c in range(9)
        ]
        blank = jnp.zeros((1, 256), F32)
        left_group = jnp.concatenate(rows[0:5] + [blank] * 3, axis=0)
        right_group = jnp.concatenate(rows[5:9] + [blank] * 4, axis=0)
        for part in range(2):
            a = left_group[:, part * LANES : (part + 1) * LANES]
            b = right_group[:, part * LANES : (part + 1) * LANES]
            even = jnp.where(lane_half, a, pltpu.roll(b, CAP, 1))
            odd = jnp.where(lane_half, pltpu.roll(a, CAP, 1), b)
            feat_out[4 * at + 2 * part] = even
            feat_out[4 * at + 2 * part + 1] = odd
        return carry

    lax.fori_loop(0, slots_all // 256, gather_body, 0)

    def feat_copy(out, into, send, recv, to, sender):
        return pltpu.make_async_remote_copy(
            src_ref=out.at[to, pl.ds(0, 5)],
            dst_ref=into.at[sender, pl.ds(0, 5)],
            send_sem=send.at[to],
            recv_sem=recv.at[sender],
            device_id=(my_view, to),
            device_id_type=MESH,
        )

    def feat_send(out, into, send, recv):
        def body(off, carry):
            feat_copy(out, into, send, recv, lax.rem(me + off, owners), me).start()
            return carry

        lax.fori_loop(1, owners, body, 0)

    def feat_wait_recv(out, into, send, recv):
        def body(off, carry):
            peer = lax.rem(me + off, owners)
            feat_copy(out, into, send, recv, peer, peer).wait_recv()
            return carry

        lax.fori_loop(1, owners, body, 0)

    def feat_wait_send(out, into, send, recv):
        def body(off, carry):
            peer = lax.rem(me + off, owners)
            feat_copy(out, into, send, recv, peer, me).wait_send()
            return carry

        lax.fori_loop(1, owners, body, 0)

    feat_send(feat_out, feat_in, feat_s, feat_r)
    feat_in[me] = feat_out[me]

    lane_row = iota((TILES, ROWS), 1)
    tile_hot = (lane_row & 15) == iota((TILES, ROWS), 0)
    tile_mask = tile_hot.astype(F32)
    entry_hot = ((iota((ENTRIES, ROWS), 1) >> 4) == iota((ENTRIES, ROWS), 0)).astype(F32).astype(BF16)
    slots = slots_ref[...]
    both = jnp.concatenate([slots >> 6, slots & (CAP - 1)], axis=0).astype(F32).astype(BF16)
    spread = dot(both, entry_hot, ((1,), (0,)))
    owner_row = jnp.sum(spread[0:TILES] * tile_mask, axis=0, keepdims=True)
    place_row = jnp.sum(spread[TILES:] * tile_mask, axis=0, keepdims=True)
    lengths = jnp.broadcast_to(len_ref[...], (TILES, TILES)).astype(F32).astype(BF16)
    len_row = dot(lengths, tile_mask.astype(BF16), ((1,), (0,)))[0:1]
    entry_row = iota((1, ROWS), 1)
    live = (entry_row >> 4).astype(F32) < len_row
    place_sub = iota((LANES, ROWS), 0)
    place_left = (place_sub.astype(F32) == place_row).astype(F32).astype(BF16)
    place_right = ((place_sub - CAP).astype(F32) == place_row).astype(F32).astype(BF16)
    center_of_x = (entry_row & 15).astype(F32) * 16.0 + (8.0 - 128.0)
    center_of_y = (me * 16 + 8 - 8 * owners).astype(F32)

    pixel = iota((8, PIXELS), 1)
    mono_x = (pixel & 15).astype(F32) - 7.5
    mono_y = (pixel >> 4).astype(F32) - 7.5
    kind = iota((8, PIXELS), 0)
    monomials = jnp.where(kind == 0, mono_x * mono_x, 0.0)
    monomials = jnp.where(kind == 1, mono_x * mono_y, monomials)
    monomials = jnp.where(kind == 2, mono_y * mono_y, monomials)
    monomials = jnp.where(kind == 3, mono_x, monomials)
    monomials = jnp.where(kind == 4, mono_y, monomials)
    monomials = jnp.where(kind == 5, 1.0, monomials)
    monomials_two = jnp.concatenate([monomials, jnp.zeros_like(monomials)], axis=0).astype(BF16)
    monomials_four = jnp.concatenate([monomials] * 3 + [jnp.zeros_like(monomials)], axis=0).astype(BF16)

    pltpu.make_async_copy(cot_ref, held_cot, load_sem.at[1]).wait()
    cot = jnp.concatenate(
        [held_cot[pl.ds(half, 3 * TILES, stride=2), :] for half in range(2)], axis=1
    )
    cot_high, cot_low = pieces(cot, 2)

    feat_wait_recv(feat_out, feat_in, feat_s, feat_r)
    arrived = feat_in[...].reshape(owners * 8, LANES)
    arrived_pieces = pieces(arrived, 3)
    left_parts = []
    right_parts = []
    for at in range(ROWS // 256):
        lanes = slice(at * 256, at * 256 + 256)
        owners_here = owner_row[:, lanes]
        totals = []
        for hot in (place_left, place_right):
            found = dot(arrived_pieces[0], hot[:, lanes], ((1,), (0,)))
            found += dot(arrived_pieces[1], hot[:, lanes], ((1,), (0,)))
            found += dot(arrived_pieces[2], hot[:, lanes], ((1,), (0,)))
            total = jnp.zeros((8, 256), F32)
            for o in range(owners):
                total = jnp.where(owners_here == float(o), found[o * 8 : o * 8 + 8], total)
            totals.append(total)
        left_parts.append(totals[0])
        right_parts.append(totals[1])
    left = jnp.concatenate(left_parts, axis=1)
    right = jnp.concatenate(right_parts, axis=1)
    center_x = left[0:1] - center_of_x
    center_y = left[1:2] - center_of_y
    conic_a = left[2:3]
    conic_b = left[3:4]
    conic_c = left[4:5]
    log_opacity = right[0:1]
    colors = [right[1 + c : 2 + c] for c in range(3)]

    lin_x = conic_a * center_x + conic_b * center_y
    lin_y = conic_b * center_x + conic_c * center_y
    blank = jnp.zeros((1, ROWS), F32)
    coefs = jnp.concatenate(
        [
            jnp.where(live, -0.5 * conic_a, 0.0),
            jnp.where(live, -conic_b, 0.0),
            jnp.where(live, -0.5 * conic_c, 0.0),
            jnp.where(live, lin_x, 0.0),
            jnp.where(live, lin_y, 0.0),
            jnp.where(live, log_opacity - 0.5 * (lin_x * center_x + lin_y * center_y), -1000.0),
            blank,
            blank,
        ],
        axis=0,
    )
    coef_pieces = jnp.concatenate(
        [piece.astype(F32) for piece in pieces(coefs, 3)] + [jnp.zeros_like(coefs)], axis=0
    )
    exponent[...] = dot(coef_pieces.T.astype(BF16), monomials_four, ((1,), (0,)))

    spread_color = jnp.concatenate([colors[c] * tile_mask for c in range(3)], axis=0)
    color_high, color_low = pieces(spread_color, 2)
    color_sides = jnp.concatenate([color_high, color_high, color_low], axis=0)
    cot_sides = jnp.concatenate([cot_high, cot_low, cot_high], axis=0)
    along[...] = dot(color_sides, cot_sides, ((0,), (0,)))

    def forward_body(k, through):
        rows = pl.ds(pl.multiple_of(k * TILES, TILES), TILES)
        alpha = jnp.exp(exponent[rows, :])
        blend = through * alpha
        alpha_all[rows, :] = alpha
        blend_all[rows, :] = blend
        high, low = pieces(blend, 2)
        split_a[rows, :] = high
        split_b[rows, :] = low
        return through - blend

    lax.fori_loop(0, ENTRIES, forward_body, jnp.ones((TILES, PIXELS), F32))

    def backward_body(step, behind):
        rows = pl.ds(pl.multiple_of((ENTRIES - 1 - step) * TILES, TILES), TILES)
        gain = along[rows, :] - behind
        high, low = pieces(blend_all[rows, :] * gain, 2)
        split_c[rows, :] = high
        split_d[rows, :] = low
        return behind + alpha_all[rows, :] * gain

    lax.fori_loop(0, ENTRIES, backward_body, jnp.zeros((TILES, PIXELS), F32))

    moments = dot(monomials_two, split_c[...], ((1,), (1,))) + dot(
        monomials_two, split_d[...], ((1,), (1,))
    )
    cot_both = jnp.concatenate([cot_high, cot_low], axis=0)
    by_color = dot(cot_both, split_a[...], ((1,), (1,)))
    by_color = (
        by_color[0 : 3 * TILES]
        + by_color[3 * TILES :]
        + dot(cot_high, split_b[...], ((1,), (1,)))
    )
    grad_colors = [
        jnp.sum(by_color[c * TILES : (c + 1) * TILES] * tile_mask, axis=0, keepdims=True)
        for c in range(3)
    ]
    m_xx, m_xy, m_yy, m_x, m_y, m_one = [moments[row : row + 1] for row in range(6)]
    off_x = m_x - center_x * m_one
    off_y = m_y - center_y * m_one
    off_xx = m_xx - center_x * (m_x + off_x)
    off_xy = m_xy - center_x * m_y - center_y * off_x
    off_yy = m_yy - center_y * (m_y + off_y)
    entry_grads = jnp.concatenate(
        [
            conic_a * off_x + conic_b * off_y,
            conic_b * off_x + conic_c * off_y,
            -0.5 * off_xx,
            -off_xy,
            -0.5 * off_yy,
            blank,
            blank,
            blank,
            m_one,
            grad_colors[0],
            grad_colors[1],
            grad_colors[2],
            blank,
            blank,
            blank,
            blank,
        ],
        axis=0,
    )
    grad_high, grad_low = pieces(entry_grads, 2)
    owner_wide = jnp.broadcast_to(owner_row, (16, ROWS)).astype(BF16)
    nothing = jnp.zeros((16, ROWS), BF16)
    for o in range(owners):
        here = owner_wide == jnp.asarray(o, BF16)
        wide[o * 16 : o * 16 + 16, 0:ROWS] = jnp.where(here, grad_high, nothing)
        wide[(owners + o) * 16 : (owners + o) * 16 + 16, 0:ROWS] = jnp.where(here, grad_low, nothing)
    place_both = place_left + place_right
    by_slot = dot(wide[0 : 32 * owners, 0:ROWS], place_both, ((1,), (1,)))
    by_slot = (by_slot[0 : 16 * owners] + by_slot[16 * owners :]).reshape(owners, 16, LANES)
    lane_half_all = iota((owners, 8, LANES), 2) < CAP
    grad_out[...] = jnp.where(lane_half_all, by_slot[:, 0:8], by_slot[:, 8:16])

    feat_send(grad_out, grad_in, grad_s, grad_r)
    grad_in[me] = grad_out[me]

    color_both = jnp.concatenate([color_high, color_low], axis=0)
    shown = dot(color_both, split_a[...], ((1,), (0,)))
    shown = (
        shown[0 : 3 * TILES]
        + shown[3 * TILES :]
        + dot(color_high, split_b[...], ((1,), (0,)))
    )
    for half in range(2):
        image[pl.ds(half, 3 * TILES, stride=2), :] = shown[:, half * LANES : half * LANES + LANES]
    pltpu.make_async_copy(image, image_ref, store_sem.at[0]).start()

    feat_wait_recv(grad_out, grad_in, grad_s, grad_r)

    def scatter_body(at, carry):
        even = grad_in[2 * at]
        odd = grad_in[2 * at + 1]
        a = jnp.where(lane_half, even, pltpu.roll(odd, CAP, 1))
        b = jnp.where(lane_half, pltpu.roll(even, CAP, 1), odd)
        lanes = pl.ds(pl.multiple_of(at * LANES, LANES), LANES)
        mask = high_hot[:, lanes].astype(BF16)
        for c in range(9):
            row = a[c : c + 1] if c < 5 else b[c - 5 : c - 4]
            for s, piece in enumerate(pieces(jnp.broadcast_to(row, (32, LANES)), 2)):
                wide[s * 288 + c * 32 : s * 288 + c * 32 + 32, lanes] = piece * mask
        return carry

    lax.fori_loop(0, slot_tiles, scatter_body, 0)
    placed = dot(wide[0:576, 0:slots_all], low_hot[...], ((1,), (1,)))
    placed = (placed[0:288] + placed[288:576]).reshape(9, 32, 256)
    dense[:, 0:32, :] = placed[:, :, 0:LANES]
    dense[:, 32:64, :] = placed[:, :, LANES:256]

    def view_copy(to, sender):
        return pltpu.make_async_remote_copy(
            src_ref=dense.at[:, pl.ds(pl.multiple_of(to * chunk, chunk), chunk), :],
            dst_ref=view_in.at[sender],
            send_sem=view_s.at[to],
            recv_sem=view_r.at[sender],
            device_id=(to, me),
            device_id_type=MESH,
        )

    def view_send(off, carry):
        view_copy(lax.rem(my_view + off, views), my_view).start()
        return carry

    lax.fori_loop(1, views, view_send, 0)
    mine = pl.ds(pl.multiple_of(my_view * chunk, chunk), chunk)
    view_in[my_view] = dense[:, mine, :]

    def cam_wait(off, carry):
        peer = lax.rem(my_view + off, views)
        cam_copy(peer, peer).wait_recv()
        cam_copy(peer, my_view).wait_send()
        return carry

    lax.fori_loop(1, views, cam_wait, 0)
    gs_wait_send(ids_out, ids_in, ids_s, ids_r)
    feat_wait_send(feat_out, feat_in, feat_s, feat_r)
    feat_wait_send(grad_out, grad_in, grad_s, grad_r)
    pltpu.make_async_copy(image, image_ref, store_sem.at[0]).wait()

    def get(r):
        return held[r, mine, :]

    scale_quat = [get(r) for r in range(3, 10)]

    def shape_of(values):
        return covariance(values[0:3], values[3:7])

    sigma, shape_back = jax.vjp(shape_of, scale_quat)
    zero = jnp.zeros((chunk, LANES), F32)
    for r in range(59):
        summed[r] = zero

    def view_wait(off, carry):
        peer = lax.rem(my_view + off, views)
        view_copy(peer, peer).wait_recv()
        view_copy(peer, my_view).wait_send()
        return carry

    lax.fori_loop(1, views, view_wait, 0)

    def view_body(v, carry):
        totals = carry
        camera = cam_in[v]
        x = get(0) - camera[0:1]
        y = get(1) - camera[1:2]
        z = get(2) - camera[2:3]
        grads = [view_in[v, c] for c in range(9)]
        _, geometry_back = jax.vjp(geometry, x, y, z, sigma)
        gx, gy, gz, g_sigma = geometry_back(tuple(grads[0:5]))
        basis, basis_back = jax.vjp(harmonic_basis, x, y, z)
        g_basis = [zero] * 15
        for c in range(3):
            color_grad = grads[6 + c]
            summed[11 + 16 * c] += sh_zero * color_grad
            for k in range(15):
                row = 12 + 16 * c + k
                summed[row] += basis[k] * color_grad
                g_basis[k] = g_basis[k] + get(row) * color_grad
        hx, hy, hz = basis_back(g_basis)
        add = [gx + hx, gy + hy, gz + hz, grads[5]] + list(g_sigma)
        return tuple(t + a for t, a in zip(totals, add))

    totals = lax.fori_loop(0, views, view_body, tuple([zero] * 10))
    for r in range(3):
        summed[r] = totals[r]
    (by_shape,) = shape_back(list(totals[4:10]))
    for r in range(7):
        summed[3 + r] = by_shape[r]
    summed[10] = totals[3] / (1.0 + jnp.exp(get(10)))

    def store_grads(j):
        return pltpu.make_async_copy(
            summed.at[:, j, :],
            grads_ref.at[:, pl.ds(pl.multiple_of(j * LANES, LANES), LANES)],
            store_sem.at[1],
        )

    def store_grads_body(j, carry):
        store_grads(j).start()
        return carry

    lax.fori_loop(0, chunk, store_grads_body, 0)
    pltpu.make_async_copy(summed, summed, store_sem.at[1]).wait()


def local(owners, views, params, cam_pos, req_ids, tile_slots, tile_len, cotangent):
    count, owned = params.shape
    blocks = owned // LANES
    chunk = blocks // views
    slots_all = owners * CAP
    vmem = pltpu.VMEM
    dma = pltpu.SemaphoreType.DMA
    whole = pl.BlockSpec(memory_space=vmem)
    image, grads = pl.pallas_call(
        functools.partial(kernel, owners, views),
        out_shape=(
            jax.ShapeDtypeStruct((6 * TILES, LANES), F32),
            jax.ShapeDtypeStruct((count, owned // views), F32),
        ),
        in_specs=[
            pl.BlockSpec(memory_space=pltpu.HBM),
            pl.BlockSpec(memory_space=pltpu.SMEM),
            whole,
            whole,
            whole,
            pl.BlockSpec(memory_space=pltpu.HBM),
        ],
        out_specs=(pl.BlockSpec(memory_space=pltpu.HBM), pl.BlockSpec(memory_space=pltpu.HBM)),
        scratch_shapes=[
            vmem((count, blocks, LANES), F32),
            vmem((6 * TILES, LANES), F32),
            vmem((6 * TILES, LANES), F32),
            vmem((count, chunk, LANES), F32),
            vmem((owners, 1, LANES), jnp.int32),
            vmem((owners, 1, LANES), jnp.int32),
            vmem((8, LANES), F32),
            vmem((views, 8, LANES), F32),
            vmem((3, 288, 256), BF16),
            vmem((256, slots_all), BF16),
            vmem((32, slots_all), F32),
            vmem((owners, 8, LANES), F32),
            vmem((owners, 8, LANES), F32),
            vmem((max(576, 32 * owners), max(ROWS, slots_all)), BF16),
            vmem((ROWS, PIXELS), F32),
            vmem((ROWS, PIXELS), F32),
            vmem((ROWS, PIXELS), F32),
            vmem((ROWS, PIXELS), F32),
            vmem((ROWS, PIXELS), BF16),
            vmem((ROWS, PIXELS), BF16),
            vmem((ROWS, PIXELS), BF16),
            vmem((ROWS, PIXELS), BF16),
            vmem((owners, 8, LANES), F32),
            vmem((owners, 8, LANES), F32),
            vmem((9, blocks, LANES), F32),
            vmem((views, 9, chunk, LANES), F32),
            dma((2,)),
            dma((2,)),
        ]
        + [dma((owners,)) for _ in range(6)]
        + [dma((views,)) for _ in range(4)],
        compiler_params=pltpu.CompilerParams(
            collective_id=0, has_side_effects=True, vmem_limit_bytes=40 * 1024 * 1024
        ),
        cost_estimate=pl.CostEstimate(
            flops=2_000_000_000, bytes_accessed=4_000_000, transcendentals=300_000
        ),
    )(
        params,
        cam_pos,
        req_ids.reshape(owners, CAP),
        tile_slots.reshape(TILES, ENTRIES),
        tile_len,
        cotangent.reshape(6 * TILES, LANES),
    )
    return image.reshape(cotangent.shape), grads


def solution(mesh):
    placed = (
        P(None, "gs"),
        P("view", None),
        P("view", "gs", None, None),
        P("view", "gs", None),
        P("view", "gs"),
        P("view", None, "gs"),
    )
    return jax.shard_map(
        functools.partial(local, mesh.shape["gs"], mesh.shape["view"]),
        mesh=mesh,
        in_specs=placed,
        out_specs=(P("view", None, "gs"), P(None, ("gs", "view"))),
        check_vma=False,
    )
```

profile of v0, /device:TPU:1, one launch (start us, length us, event | category | flops | bytes accessed | tf_op | source)
XLA Modules:
  0.0 58.5 jit_solution(2062566970972752832)
XLA Ops:
  0.6 0.0 copy-start
  0.6 1.6 %copy-done = f32[59,8192]{1,0:T(8,128)S(1)} copy-done((f32[59,8192]{1,0:T(8,128)S(1)}, f32[59,8192]{1,0:T(8,128)}, u32[]{:S(2)}) %copy-start) | copy-done | bytes 1933336
  2.2 0.0 copy-start.1
  2.2 0.8 %copy-done.1 = f32[1,3,4096]{2,0,1:T(1,128)S(1)} copy-done((f32[1,3,4096]{2,0,1:T(1,128)S(1)}, f32[1,3,4096]{2,0,1:T(1,128)}, u32[]{:S(2)}) %copy-start.1) | copy-done | bytes 49176
  3.0 0.0 copy-start.2
  3.0 0.7 %copy-done.2 = s32[1,1,32,64]{3,2,1,0:T(8,128)S(1)} copy-done((s32[1,1,32,64]{3,2,1,0:T(8,128)S(1)}, s32[1,1,32,64]{3,2,1,0:T(8,128)}, u32[]{:S(2)}) %copy-start.2) | copy-done | bytes 8216
  3.7 0.0 copy-start.3
  3.7 0.7 %copy-done.3 = s32[1,16,64]{2,1,0:T(8,128)S(1)} copy-done((s32[1,16,64]{2,1,0:T(8,128)S(1)}, s32[1,16,64]{2,1,0:T(8,128)}, u32[]{:S(2)}) %copy-start.3) | copy-done | bytes 4120
  4.4 0.0 copy-start.4
  4.4 0.7 %copy-done.4 = f32[1,3]{1,0:T(1,128)S(1)} copy-done((f32[1,3]{1,0:T(1,128)S(1)}, f32[1,3]{1,0:T(1,128)}, u32[]{:S(2)}) %copy-start.4) | copy-done | bytes 36
  5.1 0.0 copy-start.5
  5.1 0.7 %copy-done.5 = s32[1,16]{1,0:T(1,128)S(1)} copy-done((s32[1,16]{1,0:T(1,128)S(1)}, s32[1,16]{1,0:T(1,128)}, u32[]{:S(2)}) %copy-start.5) | copy-done | bytes 88
  5.7 51.4 %shard_map.77 = (f32[96,128]{1,0:T(8,128)S(1)}, f32[59,1024]{1,0:T(8,128)S(1)}) custom-call(f32[59,8192]{1,0:T(8,128)S(1)} %copy-done, f32[1,3]{1,0:T(1,128)S(1)} %copy-done.4, s32[32,64]{1,0:T(8,128)S(1)} %bitcast.6, s32[16,64]{1,0:T(8,128)S(1)} %bitcast.7, s32[1,16]{1,0:T(1,128)S(1)} %copy-done.5, f32[96,128]{1,0:T(8,128)S(1)} %bitcast.5), custom_call_target="tpu_custom_call" | custom-call | flops 2000000000 | bytes 4000000 | tf_op jit(solution)/shard_map/pallas_call | solution.py:698
  57.1 0.6 %copy.12 = f32[1,3,4096]{2,0,1:T(1,128)} copy(f32[1,3,4096]{2,0,1:T(1,128)S(1)} %bitcast.4) | data formatting | bytes 98304
  57.8 0.7 %copy.13 = f32[59,1024]{1,0:T(8,128)} copy(f32[59,1024]{1,0:T(8,128)S(1)} %get-tuple-element.13) | data formatting | bytes 483328
Async XLA Ops:
  0.6 1.6 %copy-start = (f32[59,8192]{1,0:T(8,128)S(1)}, f32[59,8192]{1,0:T(8,128)}, u32[]{:S(2)}) copy-start(f32[59,8192]{1,0:T(8,128)} %params_ref.1) | copy-start | bytes 5799940
  2.2 0.8 %copy-start.1 = (f32[1,3,4096]{2,0,1:T(1,128)S(1)}, f32[1,3,4096]{2,0,1:T(1,128)}, u32[]{:S(2)}) copy-start(f32[1,3,4096]{2,0,1:T(1,128)} %param.11) | copy-start | bytes 147460
  3.0 0.7 %copy-start.2 = (s32[1,1,32,64]{3,2,1,0:T(8,128)S(1)}, s32[1,1,32,64]{3,2,1,0:T(8,128)}, u32[]{:S(2)}) copy-start(s32[1,1,32,64]{3,2,1,0:T(8,128)} %param.8) | copy-start | bytes 24580
  3.7 0.7 %copy-start.3 = (s32[1,16,64]{2,1,0:T(8,128)S(1)}, s32[1,16,64]{2,1,0:T(8,128)}, u32[]{:S(2)}) copy-start(s32[1,16,64]{2,1,0:T(8,128)} %param.9) | copy-start | bytes 12292
  4.4 0.7 %copy-start.4 = (f32[1,3]{1,0:T(1,128)S(1)}, f32[1,3]{1,0:T(1,128)}, u32[]{:S(2)}) copy-start(f32[1,3]{1,0:T(1,128)} %cam_ref.1) | copy-start | bytes 40
  5.1 0.7 %copy-start.5 = (s32[1,16]{1,0:T(1,128)S(1)}, s32[1,16]{1,0:T(1,128)}, u32[]{:S(2)}) copy-start(s32[1,16]{1,0:T(1,128)} %len_ref.1) | copy-start | bytes 196
where the time goes:
time: 58.7 us; the launch traced here: 58.5 us
  Pallas kernels  51.4 us (88%)
  local copies, waits for them, and re-layouts  6.43 us (11%)
  between operations  0.65 us (1%)
    pallas_call x1, Pallas kernels, local(): pl.pallas_call(functools.partial(kernel, owners, views), out_shape=(jax.S...  51.4 us
    unnamed x14, local copies, waits for them, and re-layouts  6.43 us

commit v1 on v0

--- a/solution.py
+++ b/solution.py
@@ -16,6 +16,7 @@
 PIXELS = 256
 CAP = 64
 LANES = 128
+LINE = 4
 
 focal = 1.2 * 128.0
 dilate = 0.3
@@ -137,6 +138,10 @@
     image_ref,
     grads_ref,
     held,
+    asked,
+    cam_held,
+    slots_held,
+    len_held,
     held_cot,
     image,
     summed,
@@ -150,6 +155,7 @@
     feat_out,
     feat_in,
     wide,
+    gathered,
     exponent,
     along,
     alpha_all,
@@ -177,91 +183,93 @@
 ):
     me = lax.axis_index("gs")
     my_view = lax.axis_index("view")
+    my_y = lax.rem(me, LINE)
+    my_z = lax.div(me, LINE)
+    my_x = lax.div(my_view, 2)
+    my_core = lax.rem(my_view, 2)
+    planes = owners // LINE
     blocks = held.shape[1]
     chunk = blocks // views
-    slots_all = owners * CAP
-    slot_tiles = slots_all // LANES
-
-    def load(j):
-        return pltpu.make_async_copy(
+
+    def plane(i):
+        half = (i + 1) // 2
+        odd = i % 2
+        return lax.rem(my_z + odd * half + (1 - odd) * (planes - half), planes)
+
+    def peers(i, first):
+        return [plane(i) * LINE + lax.rem(my_y + step, LINE) for step in range(1 if first else 0, LINE)]
+
+    def view_peer(i):
+        pair = i // 2
+        step = pair + pair // 2 - 2 * (pair // 3)
+        return lax.rem(my_x + step, views // 2) * 2 + lax.rem(my_core + i, 2)
+
+    ids_load = pltpu.make_async_copy(ids_ref.at[0, 0], asked, load_sem.at[2])
+    cam_load = pltpu.make_async_copy(cam_ref, cam_held, load_sem.at[3])
+    slots_load = pltpu.make_async_copy(slots_ref.at[0], slots_held, load_sem.at[4])
+    len_load = pltpu.make_async_copy(len_ref, len_held, load_sem.at[5])
+    cot_load = pltpu.make_async_copy(cot_ref, held_cot, load_sem.at[1])
+    ids_load.start()
+    cam_load.start()
+
+    barrier = pltpu.get_barrier_semaphore()
+
+    def greet(off, carry):
+        peer = lax.rem(me + off, owners)
+        pl.semaphore_signal(barrier, inc=1, device_id=(my_view, peer), device_id_type=MESH)
+        return carry
+
+    lax.fori_loop(1, owners, greet, 0)
+
+    def greet_view(off, carry):
+        peer = lax.rem(my_view + off, views)
+        pl.semaphore_signal(barrier, inc=1, device_id=(peer, me), device_id_type=MESH)
+        return carry
+
+    lax.fori_loop(1, views, greet_view, 0)
+
+    def load_body(j, carry):
+        pltpu.make_async_copy(
             params_ref.at[:, pl.ds(pl.multiple_of(j * LANES, LANES), LANES)],
             held.at[:, j, :],
             load_sem.at[0],
-        )
-
-    def load_body(j, carry):
-        load(j).start()
+        ).start()
         return carry
 
     lax.fori_loop(0, blocks, load_body, 0)
-
-    pltpu.make_async_copy(cot_ref, held_cot, load_sem.at[1]).start()
-
-    barrier = pltpu.get_barrier_semaphore()
-
-    def greet(off, carry):
-        peer = lax.rem(me + off, owners)
-        pl.semaphore_signal(barrier, inc=1, device_id=(my_view, peer), device_id_type=MESH)
-        return carry
-
-    lax.fori_loop(1, owners, greet, 0)
-
-    def greet_view(off, carry):
-        peer = lax.rem(my_view + off, views)
-        pl.semaphore_signal(barrier, inc=1, device_id=(peer, me), device_id_type=MESH)
-        return carry
-
-    lax.fori_loop(1, views, greet_view, 0)
-
-    def gs_copy(out, into, send, recv, to, sender):
+    slots_load.start()
+    len_load.start()
+    cot_load.start()
+
+    def ids_copy(to, sender):
         return pltpu.make_async_remote_copy(
-            src_ref=out.at[to],
-            dst_ref=into.at[sender],
-            send_sem=send.at[to],
-            recv_sem=recv.at[sender],
+            src_ref=ids_out.at[to],
+            dst_ref=ids_in.at[sender],
+            send_sem=ids_s.at[to],
+            recv_sem=ids_r.at[sender],
             device_id=(my_view, to),
             device_id_type=MESH,
         )
 
-    def gs_send(out, into, send, recv):
-        def body(off, carry):
-            peer = lax.rem(me + off, owners)
-            gs_copy(out, into, send, recv, peer, me).start()
-            return carry
-
-        lax.fori_loop(1, owners, body, 0)
-
-    def gs_wait_recv(out, into, send, recv):
-        def body(off, carry):
-            peer = lax.rem(me + off, owners)
-            gs_copy(out, into, send, recv, peer, peer).wait_recv()
-            return carry
-
-        lax.fori_loop(1, owners, body, 0)
-
-    def gs_wait_send(out, into, send, recv):
-        def body(off, carry):
-            peer = lax.rem(me + off, owners)
-            gs_copy(out, into, send, recv, peer, me).wait_send()
-            return carry
-
-        lax.fori_loop(1, owners, body, 0)
-
-    asked = ids_ref[...]
-    doubled = jnp.concatenate([asked, asked], axis=1)
-    my_half = (iota(doubled.shape, 1) >> 6) == lax.rem(me, 2)
-    ids_out[...] = jnp.where(my_half, doubled, 0).reshape(owners, 1, LANES)
-    cam_x = cam_ref[0, 0]
-    cam_y = cam_ref[0, 1]
-    cam_z = cam_ref[0, 2]
-    cam_row = iota((8, LANES), 0)
-    cam_tile = jnp.where(cam_row == 0, cam_x, jnp.where(cam_row == 1, cam_y, cam_z))
-    cam_out[...] = cam_tile
-
-    pl.semaphore_wait(barrier, owners + views - 2)
-
-    gs_send(ids_out, ids_in, ids_s, ids_r)
-    ids_in[me] = ids_out[me]
+    def feat_copy(to, sender):
+        return pltpu.make_async_remote_copy(
+            src_ref=feat_out.at[to, pl.ds(0, 5)],
+            dst_ref=feat_in.at[sender, pl.ds(0, 5)],
+            send_sem=feat_s.at[to],
+            recv_sem=feat_r.at[sender],
+            device_id=(my_view, to),
+            device_id_type=MESH,
+        )
+
+    def grad_copy(to, sender):
+        return pltpu.make_async_remote_copy(
+            src_ref=grad_out.at[to, pl.ds(0, 5)],
+            dst_ref=grad_in.at[sender, pl.ds(0, 5)],
+            send_sem=grad_s.at[to],
+            recv_sem=grad_r.at[sender],
+            device_id=(my_view, to),
+            device_id_type=MESH,
+        )
 
     def cam_copy(to, sender):
         return pltpu.make_async_remote_copy(
@@ -273,11 +281,34 @@
             device_id_type=MESH,
         )
 
-    def cam_send(off, carry):
-        cam_copy(lax.rem(my_view + off, views), my_view).start()
-        return carry
-
-    lax.fori_loop(1, views, cam_send, 0)
+    def view_copy(to, sender):
+        return pltpu.make_async_remote_copy(
+            src_ref=dense.at[:, pl.ds(pl.multiple_of(to * chunk, chunk), chunk), :],
+            dst_ref=view_in.at[sender],
+            send_sem=view_s.at[to],
+            recv_sem=view_r.at[sender],
+            device_id=(to, me),
+            device_id_type=MESH,
+        )
+
+    def wait_sent(copy):
+        def body(off, carry):
+            copy(lax.rem(me + off, owners), me).wait_send()
+            return carry
+
+        lax.fori_loop(1, owners, body, 0)
+
+    ids_load.wait()
+    doubled = jnp.concatenate([asked[...], asked[...]], axis=1)
+    my_half = (iota(doubled.shape, 1) >> 6) == lax.rem(me, 2)
+    ids_out[...] = jnp.where(my_half, doubled, 0).reshape(owners, 1, LANES)
+    ids_in[me] = ids_out[me]
+    cam_load.wait()
+    cam_row = iota((8, LANES), 0)
+    cam_tile = jnp.where(
+        cam_row == 0, cam_held[0:1, 0:1], jnp.where(cam_row == 1, cam_held[0:1, 1:2], cam_held[0:1, 2:3])
+    )
+    cam_out[...] = cam_tile
     cam_in[my_view] = cam_tile
 
     pltpu.make_async_copy(held, held, load_sem.at[0]).wait()
@@ -288,9 +319,9 @@
         def get(r):
             return held[r, rows, :]
 
-        x = get(0) - cam_x
-        y = get(1) - cam_y
-        z = get(2) - cam_z
+        x = get(0) - cam_out[0:1]
+        y = get(1) - cam_out[1:2]
+        z = get(2) - cam_out[2:3]
         sigma = covariance([get(3), get(4), get(5)], [get(6), get(7), get(8), get(9)])
         values = list(geometry(x, y, z, sigma))
         values.append(-jnp.log(1.0 + jnp.exp(-get(10))))
@@ -310,91 +341,76 @@
 
     lax.fori_loop(0, blocks // 16, features_body, 0)
 
-    gs_wait_recv(ids_out, ids_in, ids_s, ids_r)
-
-    def hot_body(at, carry):
-        ids = ids_in[2 * at] + ids_in[2 * at + 1]
+    pl.semaphore_wait(barrier, owners + views - 2)
+
+    def ids_body(step, carry):
+        for peer in peers(planes - 1 - step, False):
+            ids_copy(peer, me).start()
+        return carry
+
+    lax.fori_loop(0, planes - 1, ids_body, 0)
+    for peer in peers(0, True):
+        ids_copy(peer, me).start()
+
+    def cam_send(off, carry):
+        cam_copy(lax.rem(my_view + off, views), my_view).start()
+        return carry
+
+    lax.fori_loop(1, views, cam_send, 0)
+
+    lane_half = iota((8, LANES), 1) < CAP
+
+    def serve(i, first):
+        for peer in peers(i, first):
+            ids_copy(peer, peer).wait_recv()
+        base = plane(i) * LINE
+        ids = jnp.concatenate(
+            [ids_in[base] + ids_in[base + 1], ids_in[base + 2] + ids_in[base + 3]], axis=1
+        )
         low = (ids & (LANES - 1)) + ((ids >> 12) << 7)
         high = (ids >> 7) & 31
-        lanes = pl.ds(pl.multiple_of(at * LANES, LANES), LANES)
-        low_hot[:, lanes] = (iota((256, LANES), 0) == low).astype(F32).astype(BF16)
-        high_hot[:, lanes] = (iota((32, LANES), 0) == high).astype(F32)
-        return carry
-
-    lax.fori_loop(0, slot_tiles, hot_body, 0)
-
-    lane_half = iota((8, LANES), 1) < CAP
-
-    def gather_body(at, carry):
-        lanes = pl.ds(pl.multiple_of(at * 256, 256), 256)
-        right = low_hot[:, lanes]
+        lanes = pl.ds(pl.multiple_of(base * CAP, LINE * CAP), LINE * CAP)
+        right = (iota((256, LINE * CAP), 0) == low).astype(F32).astype(BF16)
+        low_hot[:, lanes] = right
+        mask = (iota((32, LINE * CAP), 0) == high).astype(F32)
+        high_hot[:, lanes] = mask.astype(BF16)
         picked = dot(table[0], right, ((1,), (0,)))
         picked += dot(table[1], right, ((1,), (0,)))
         picked += dot(table[2], right, ((1,), (0,)))
-        mask = high_hot[:, lanes]
         rows = [
             jnp.sum(picked[c * 32 : c * 32 + 32] * mask, axis=0, keepdims=True) for c in range(9)
         ]
-        blank = jnp.zeros((1, 256), F32)
+        blank = jnp.zeros((1, LINE * CAP), F32)
         left_group = jnp.concatenate(rows[0:5] + [blank] * 3, axis=0)
         right_group = jnp.concatenate(rows[5:9] + [blank] * 4, axis=0)
         for part in range(2):
             a = left_group[:, part * LANES : (part + 1) * LANES]
             b = right_group[:, part * LANES : (part + 1) * LANES]
-            even = jnp.where(lane_half, a, pltpu.roll(b, CAP, 1))
-            odd = jnp.where(lane_half, pltpu.roll(a, CAP, 1), b)
-            feat_out[4 * at + 2 * part] = even
-            feat_out[4 * at + 2 * part + 1] = odd
-        return carry
-
-    lax.fori_loop(0, slots_all // 256, gather_body, 0)
-
-    def feat_copy(out, into, send, recv, to, sender):
-        return pltpu.make_async_remote_copy(
-            src_ref=out.at[to, pl.ds(0, 5)],
-            dst_ref=into.at[sender, pl.ds(0, 5)],
-            send_sem=send.at[to],
-            recv_sem=recv.at[sender],
-            device_id=(my_view, to),
-            device_id_type=MESH,
-        )
-
-    def feat_send(out, into, send, recv):
-        def body(off, carry):
-            feat_copy(out, into, send, recv, lax.rem(me + off, owners), me).start()
-            return carry
-
-        lax.fori_loop(1, owners, body, 0)
-
-    def feat_wait_recv(out, into, send, recv):
-        def body(off, carry):
-            peer = lax.rem(me + off, owners)
-            feat_copy(out, into, send, recv, peer, peer).wait_recv()
-            return carry
-
-        lax.fori_loop(1, owners, body, 0)
-
-    def feat_wait_send(out, into, send, recv):
-        def body(off, carry):
-            peer = lax.rem(me + off, owners)
-            feat_copy(out, into, send, recv, peer, me).wait_send()
-            return carry
-
-        lax.fori_loop(1, owners, body, 0)
-
-    feat_send(feat_out, feat_in, feat_s, feat_r)
+            feat_out[base + 2 * part] = jnp.where(lane_half, a, pltpu.roll(b, CAP, 1))
+            feat_out[base + 2 * part + 1] = jnp.where(lane_half, pltpu.roll(a, CAP, 1), b)
+        for peer in peers(i, first):
+            feat_copy(peer, me).start()
+
+    def serve_body(i, carry):
+        serve(i, False)
+        return carry
+
+    serve(0, True)
+    lax.fori_loop(1, planes, serve_body, 0)
     feat_in[me] = feat_out[me]
 
+    slots_load.wait()
+    len_load.wait()
     lane_row = iota((TILES, ROWS), 1)
     tile_hot = (lane_row & 15) == iota((TILES, ROWS), 0)
     tile_mask = tile_hot.astype(F32)
     entry_hot = ((iota((ENTRIES, ROWS), 1) >> 4) == iota((ENTRIES, ROWS), 0)).astype(F32).astype(BF16)
-    slots = slots_ref[...]
+    slots = slots_held[...]
     both = jnp.concatenate([slots >> 6, slots & (CAP - 1)], axis=0).astype(F32).astype(BF16)
     spread = dot(both, entry_hot, ((1,), (0,)))
     owner_row = jnp.sum(spread[0:TILES] * tile_mask, axis=0, keepdims=True)
     place_row = jnp.sum(spread[TILES:] * tile_mask, axis=0, keepdims=True)
-    lengths = jnp.broadcast_to(len_ref[...], (TILES, TILES)).astype(F32).astype(BF16)
+    lengths = jnp.broadcast_to(len_held[...], (TILES, TILES)).astype(F32).astype(BF16)
     len_row = dot(lengths, tile_mask.astype(BF16), ((1,), (0,)))[0:1]
     entry_row = iota((1, ROWS), 1)
     live = (entry_row >> 4).astype(F32) < len_row
@@ -417,33 +433,44 @@
     monomials_two = jnp.concatenate([monomials, jnp.zeros_like(monomials)], axis=0).astype(BF16)
     monomials_four = jnp.concatenate([monomials] * 3 + [jnp.zeros_like(monomials)], axis=0).astype(BF16)
 
-    pltpu.make_async_copy(cot_ref, held_cot, load_sem.at[1]).wait()
+    cot_load.wait()
     cot = jnp.concatenate(
         [held_cot[pl.ds(half, 3 * TILES, stride=2), :] for half in range(2)], axis=1
     )
     cot_high, cot_low = pieces(cot, 2)
 
-    feat_wait_recv(feat_out, feat_in, feat_s, feat_r)
-    arrived = feat_in[...].reshape(owners * 8, LANES)
-    arrived_pieces = pieces(arrived, 3)
-    left_parts = []
-    right_parts = []
-    for at in range(ROWS // 256):
-        lanes = slice(at * 256, at * 256 + 256)
-        owners_here = owner_row[:, lanes]
-        totals = []
-        for hot in (place_left, place_right):
-            found = dot(arrived_pieces[0], hot[:, lanes], ((1,), (0,)))
-            found += dot(arrived_pieces[1], hot[:, lanes], ((1,), (0,)))
-            found += dot(arrived_pieces[2], hot[:, lanes], ((1,), (0,)))
-            total = jnp.zeros((8, 256), F32)
-            for o in range(owners):
-                total = jnp.where(owners_here == float(o), found[o * 8 : o * 8 + 8], total)
-            totals.append(total)
-        left_parts.append(totals[0])
-        right_parts.append(totals[1])
-    left = jnp.concatenate(left_parts, axis=1)
-    right = jnp.concatenate(right_parts, axis=1)
+    halves = [[jnp.zeros((8, 256), F32)] * (ROWS // 256) for _ in range(2)]
+
+    def collect(group):
+        for i in group:
+            for peer in peers(i, i == 0):
+                feat_copy(peer, peer).wait_recv()
+        bases = [plane(i) * LINE for i in group]
+        arrived = jnp.concatenate(
+            [feat_in[pl.ds(base, LINE)].reshape(LINE * 8, LANES) for base in bases], axis=0
+        )
+        count = arrived.shape[0]
+        stack = jnp.concatenate(pieces(arrived, 3), axis=0)
+        for at in range(ROWS // 256):
+            lanes = slice(at * 256, at * 256 + 256)
+            owners_here = owner_row[:, lanes]
+            for side, hot in enumerate((place_left, place_right)):
+                found = dot(stack, hot[:, lanes], ((1,), (0,)))
+                found = found[0:count] + found[count : 2 * count] + found[2 * count :]
+                total = halves[side][at]
+                for n, base in enumerate(bases):
+                    for step in range(LINE):
+                        row = (n * LINE + step) * 8
+                        here = owners_here == (base + step).astype(F32)
+                        total = jnp.where(here, found[row : row + 8], total)
+                halves[side][at] = total
+
+    near = (planes * 5 + 7) // 8
+    collect(list(range(near)))
+    if near < planes:
+        collect(list(range(near, planes)))
+    left = jnp.concatenate(halves[0], axis=1)
+    right = jnp.concatenate(halves[1], axis=1)
     center_x = left[0:1] - center_of_x
     center_y = left[1:2] - center_of_y
     conic_a = left[2:3]
@@ -544,19 +571,33 @@
         axis=0,
     )
     grad_high, grad_low = pieces(entry_grads, 2)
+
+    place_both = place_left + place_right
     owner_wide = jnp.broadcast_to(owner_row, (16, ROWS)).astype(BF16)
     nothing = jnp.zeros((16, ROWS), BF16)
-    for o in range(owners):
-        here = owner_wide == jnp.asarray(o, BF16)
-        wide[o * 16 : o * 16 + 16, 0:ROWS] = jnp.where(here, grad_high, nothing)
-        wide[(owners + o) * 16 : (owners + o) * 16 + 16, 0:ROWS] = jnp.where(here, grad_low, nothing)
-    place_both = place_left + place_right
-    by_slot = dot(wide[0 : 32 * owners, 0:ROWS], place_both, ((1,), (1,)))
-    by_slot = (by_slot[0 : 16 * owners] + by_slot[16 * owners :]).reshape(owners, 16, LANES)
-    lane_half_all = iota((owners, 8, LANES), 2) < CAP
-    grad_out[...] = jnp.where(lane_half_all, by_slot[:, 0:8], by_slot[:, 8:16])
-
-    feat_send(grad_out, grad_in, grad_s, grad_r)
+    lane_half_all = iota((LINE, 8, LANES), 2) < CAP
+
+    def give(group):
+        parts = []
+        for piece in (grad_high, grad_low):
+            for i in group:
+                for step in range(LINE):
+                    here = owner_wide == (plane(i) * LINE + step).astype(F32).astype(BF16)
+                    parts.append(jnp.where(here, piece, nothing))
+        by_slot = dot(jnp.concatenate(parts, axis=0), place_both, ((1,), (1,)))
+        half_rows = 16 * LINE * len(group)
+        by_slot = by_slot[0:half_rows] + by_slot[half_rows:]
+        for n, i in enumerate(group):
+            mine = by_slot[n * LINE * 16 : (n + 1) * LINE * 16].reshape(LINE, 16, LANES)
+            packed = jnp.where(lane_half_all, mine[:, 0:8], mine[:, 8:16])
+            grad_out[pl.ds(plane(i) * LINE, LINE)] = packed
+        for i in group:
+            for peer in peers(i, i == 0):
+                grad_copy(peer, me).start()
+
+    order = list(range(planes))[::-1]
+    for at in range(0, planes, 2):
+        give(order[at : at + 2])
     grad_in[me] = grad_out[me]
 
     color_both = jnp.concatenate([color_high, color_low], axis=0)
@@ -570,42 +611,50 @@
         image[pl.ds(half, 3 * TILES, stride=2), :] = shown[:, half * LANES : half * LANES + LANES]
     pltpu.make_async_copy(image, image_ref, store_sem.at[0]).start()
 
-    feat_wait_recv(grad_out, grad_in, grad_s, grad_r)
-
-    def scatter_body(at, carry):
-        even = grad_in[2 * at]
-        odd = grad_in[2 * at + 1]
-        a = jnp.where(lane_half, even, pltpu.roll(odd, CAP, 1))
-        b = jnp.where(lane_half, pltpu.roll(even, CAP, 1), odd)
-        lanes = pl.ds(pl.multiple_of(at * LANES, LANES), LANES)
-        mask = high_hot[:, lanes].astype(BF16)
+    wait_sent(ids_copy)
+    wait_sent(feat_copy)
+
+    def scatter(i, first):
+        for peer in peers(i, first):
+            grad_copy(peer, peer).wait_recv()
+        base = plane(i) * LINE
+        lanes = pl.ds(pl.multiple_of(base * CAP, LINE * CAP), LINE * CAP)
+        tops = []
+        bottoms = []
+        for part in range(2):
+            even = grad_in[base + 2 * part]
+            odd = grad_in[base + 2 * part + 1]
+            tops.append(jnp.where(lane_half, even, pltpu.roll(odd, CAP, 1)))
+            bottoms.append(jnp.where(lane_half, pltpu.roll(even, CAP, 1), odd))
+        a = jnp.concatenate(tops, axis=1)
+        b = jnp.concatenate(bottoms, axis=1)
+        mask = high_hot[:, lanes]
         for c in range(9):
             row = a[c : c + 1] if c < 5 else b[c - 5 : c - 4]
-            for s, piece in enumerate(pieces(jnp.broadcast_to(row, (32, LANES)), 2)):
-                wide[s * 288 + c * 32 : s * 288 + c * 32 + 32, lanes] = piece * mask
-        return carry
-
-    lax.fori_loop(0, slot_tiles, scatter_body, 0)
-    placed = dot(wide[0:576, 0:slots_all], low_hot[...], ((1,), (1,)))
-    placed = (placed[0:288] + placed[288:576]).reshape(9, 32, 256)
+            for s, piece in enumerate(pieces(jnp.broadcast_to(row, (32, LINE * CAP)), 2)):
+                wide[s * 288 + c * 32 : s * 288 + c * 32 + 32, :] = piece * mask
+        placed = dot(wide[...], low_hot[:, lanes], ((1,), (1,)))
+        placed = placed[0:288] + placed[288:576]
+        if first:
+            gathered[...] = placed
+        else:
+            gathered[...] += placed
+
+    def scatter_body(i, carry):
+        scatter(i, False)
+        return carry
+
+    scatter(0, True)
+    lax.fori_loop(1, planes, scatter_body, 0)
+    placed = gathered[...].reshape(9, 32, 256)
     dense[:, 0:32, :] = placed[:, :, 0:LANES]
     dense[:, 32:64, :] = placed[:, :, LANES:256]
 
-    def view_copy(to, sender):
-        return pltpu.make_async_remote_copy(
-            src_ref=dense.at[:, pl.ds(pl.multiple_of(to * chunk, chunk), chunk), :],
-            dst_ref=view_in.at[sender],
-            send_sem=view_s.at[to],
-            recv_sem=view_r.at[sender],
-            device_id=(to, me),
-            device_id_type=MESH,
-        )
-
-    def view_send(off, carry):
-        view_copy(lax.rem(my_view + off, views), my_view).start()
-        return carry
-
-    lax.fori_loop(1, views, view_send, 0)
+    def view_send(step, carry):
+        view_copy(view_peer(views - 1 - step), my_view).start()
+        return carry
+
+    lax.fori_loop(0, views - 1, view_send, 0)
     mine = pl.ds(pl.multiple_of(my_view * chunk, chunk), chunk)
     view_in[my_view] = dense[:, mine, :]
 
@@ -616,9 +665,7 @@
         return carry
 
     lax.fori_loop(1, views, cam_wait, 0)
-    gs_wait_send(ids_out, ids_in, ids_s, ids_r)
-    feat_wait_send(feat_out, feat_in, feat_s, feat_r)
-    feat_wait_send(grad_out, grad_in, grad_s, grad_r)
+    wait_sent(grad_copy)
     pltpu.make_async_copy(image, image_ref, store_sem.at[0]).wait()
 
     def get(r):
@@ -634,16 +681,7 @@
     for r in range(59):
         summed[r] = zero
 
-    def view_wait(off, carry):
-        peer = lax.rem(my_view + off, views)
-        view_copy(peer, peer).wait_recv()
-        view_copy(peer, my_view).wait_send()
-        return carry
-
-    lax.fori_loop(1, views, view_wait, 0)
-
-    def view_body(v, carry):
-        totals = carry
+    def add_view(v, totals):
         camera = cam_in[v]
         x = get(0) - camera[0:1]
         y = get(1) - camera[1:2]
@@ -664,7 +702,13 @@
         add = [gx + hx, gy + hy, gz + hz, grads[5]] + list(g_sigma)
         return tuple(t + a for t, a in zip(totals, add))
 
-    totals = lax.fori_loop(0, views, view_body, tuple([zero] * 10))
+    def view_body(i, totals):
+        peer = view_peer(i)
+        view_copy(peer, peer).wait_recv()
+        return add_view(peer, totals)
+
+    totals = add_view(my_view, tuple([zero] * 10))
+    totals = lax.fori_loop(1, views, view_body, totals)
     for r in range(3):
         summed[r] = totals[r]
     (by_shape,) = shape_back(list(totals[4:10]))
@@ -684,6 +728,12 @@
         return carry
 
     lax.fori_loop(0, chunk, store_grads_body, 0)
+
+    def view_wait(off, carry):
+        view_copy(lax.rem(my_view + off, views), my_view).wait_send()
+        return carry
+
+    lax.fori_loop(1, views, view_wait, 0)
     pltpu.make_async_copy(summed, summed, store_sem.at[1]).wait()
 
 
@@ -694,24 +744,21 @@
     slots_all = owners * CAP
     vmem = pltpu.VMEM
     dma = pltpu.SemaphoreType.DMA
-    whole = pl.BlockSpec(memory_space=vmem)
+    anywhere = pl.BlockSpec(memory_space=pl.ANY)
     image, grads = pl.pallas_call(
         functools.partial(kernel, owners, views),
         out_shape=(
             jax.ShapeDtypeStruct((6 * TILES, LANES), F32),
             jax.ShapeDtypeStruct((count, owned // views), F32),
         ),
-        in_specs=[
-            pl.BlockSpec(memory_space=pltpu.HBM),
-            pl.BlockSpec(memory_space=pltpu.SMEM),
-            whole,
-            whole,
-            whole,
-            pl.BlockSpec(memory_space=pltpu.HBM),
-        ],
-        out_specs=(pl.BlockSpec(memory_space=pltpu.HBM), pl.BlockSpec(memory_space=pltpu.HBM)),
+        in_specs=[anywhere] * 6,
+        out_specs=(anywhere, anywhere),
         scratch_shapes=[
             vmem((count, blocks, LANES), F32),
+            vmem((owners, CAP), jnp.int32),
+            vmem((1, 3), F32),
+            vmem((TILES, ENTRIES), jnp.int32),
+            vmem((1, TILES), jnp.int32),
             vmem((6 * TILES, LANES), F32),
             vmem((6 * TILES, LANES), F32),
             vmem((count, chunk, LANES), F32),
@@ -721,10 +768,11 @@
             vmem((views, 8, LANES), F32),
             vmem((3, 288, 256), BF16),
             vmem((256, slots_all), BF16),
-            vmem((32, slots_all), F32),
+            vmem((32, slots_all), BF16),
             vmem((owners, 8, LANES), F32),
             vmem((owners, 8, LANES), F32),
-            vmem((max(576, 32 * owners), max(ROWS, slots_all)), BF16),
+            vmem((576, LINE * CAP), BF16),
+            vmem((288, 256), F32),
             vmem((ROWS, PIXELS), F32),
             vmem((ROWS, PIXELS), F32),
             vmem((ROWS, PIXELS), F32),
@@ -737,13 +785,13 @@
             vmem((owners, 8, LANES), F32),
             vmem((9, blocks, LANES), F32),
             vmem((views, 9, chunk, LANES), F32),
-            dma((2,)),
+            dma((6,)),
             dma((2,)),
         ]
         + [dma((owners,)) for _ in range(6)]
         + [dma((views,)) for _ in range(4)],
         compiler_params=pltpu.CompilerParams(
-            collective_id=0, has_side_effects=True, vmem_limit_bytes=40 * 1024 * 1024
+            collective_id=0, has_side_effects=True, vmem_limit_bytes=60 * 1024 * 1024
         ),
         cost_estimate=pl.CostEstimate(
             flops=2_000_000_000, bytes_accessed=4_000_000, transcendentals=300_000
@@ -751,8 +799,8 @@
     )(
         params,
         cam_pos,
-        req_ids.reshape(owners, CAP),
-        tile_slots.reshape(TILES, ENTRIES),
+        req_ids,
+        tile_slots,
         tile_len,
         cotangent.reshape(6 * TILES, LANES),
     )

time: 58.7 us -> 45.8 us (0.78)
  Pallas kernels: 51.4 us -> 41.8 us
  local copies, waits for them, and re-layouts: 6.43 us -> 3.09 us
    pallas_call x1, Pallas kernels: 51.4 us -> 41.8 us  [local(): pl.pallas_call(functools.partial(kernel, owners, views), out_shape=(jax.S...]
    unnamed x14 -> x2, local copies, waits for them, and re-layouts: 6.43 us -> 3.09 us
where the time goes in v1:
time: 45.8 us; the launch traced here: 45.5 us
  Pallas kernels  41.8 us (91%)
  local copies, waits for them, and re-layouts  3.09 us (7%)
  between operations  0.64 us (1%)
    pallas_call x1, Pallas kernels, local(): pl.pallas_call(functools.partial(kernel, owners, views), out_shape=(jax.S...  41.8 us
    unnamed x2, local copies, waits for them, and re-layouts  3.09 us

profile of v1, /device:TPU:1, one launch (start us, length us, event | category | flops | bytes accessed | tf_op | source)
XLA Modules:
  0.0 45.5 jit_solution(1104692390095680152)
XLA Ops:
  0.6 41.8 %shard_map.77 = (f32[96,128]{1,0:T(8,128)}, f32[59,1024]{1,0:T(8,128)}) custom-call(f32[59,8192]{1,0:T(8,128)} %params_ref.1, f32[1,3]{1,0:T(1,128)} %cam_ref.1, s32[1,1,32,64]{3,2,1,0:T(8,128)} %ids_ref.1, s32[1,16,64]{2,1,0:T(8,128)} %slots_ref.1, s32[1,16]{1,0:T(1,128)} %len_ref.1, f32[96,128]{1,0:T(8,128)} %bitcast.3), custom_call_target="tpu_custom_call" | custom-call | flops 2000000000 | bytes 4000000 | tf_op jit(solution)/shard_map/pallas_call | solution.py:748
  42.4 1.4 %copy.12 = f32[1,3,4096]{2,0,1:T(1,128)} copy(f32[1,3,4096]{2,0,1:T(1,128)} %bitcast.2) | data formatting | bytes 98304
  43.8 1.7 %copy.13 = f32[59,1024]{1,0:T(8,128)} copy(f32[59,1024]{1,0:T(8,128)} %get-tuple-element.13) | data formatting | bytes 483328

commit v2 on v1

--- a/solution.py
+++ b/solution.py
@@ -311,6 +311,23 @@
     cam_out[...] = cam_tile
     cam_in[my_view] = cam_tile
 
+    pl.semaphore_wait(barrier, owners + views - 2)
+
+    def ids_body(step, carry):
+        for peer in peers(planes - 1 - step, False):
+            ids_copy(peer, me).start()
+        return carry
+
+    lax.fori_loop(0, planes - 1, ids_body, 0)
+    for peer in peers(0, True):
+        ids_copy(peer, me).start()
+
+    def cam_send(off, carry):
+        cam_copy(lax.rem(my_view + off, views), my_view).start()
+        return carry
+
+    lax.fori_loop(1, views, cam_send, 0)
+
     pltpu.make_async_copy(held, held, load_sem.at[0]).wait()
 
     def features_body(at, carry):
@@ -341,23 +358,6 @@
 
     lax.fori_loop(0, blocks // 16, features_body, 0)
 
-    pl.semaphore_wait(barrier, owners + views - 2)
-
-    def ids_body(step, carry):
-        for peer in peers(planes - 1 - step, False):
-            ids_copy(peer, me).start()
-        return carry
-
-    lax.fori_loop(0, planes - 1, ids_body, 0)
-    for peer in peers(0, True):
-        ids_copy(peer, me).start()
-
-    def cam_send(off, carry):
-        cam_copy(lax.rem(my_view + off, views), my_view).start()
-        return carry
-
-    lax.fori_loop(1, views, cam_send, 0)
-
     lane_half = iota((8, LANES), 1) < CAP
 
     def serve(i, first):
@@ -376,7 +376,8 @@
         high_hot[:, lanes] = mask.astype(BF16)
         picked = dot(table[0], right, ((1,), (0,)))
         picked += dot(table[1], right, ((1,), (0,)))
-        picked += dot(table[2], right, ((1,), (0,)))
+        rest = dot(table[2, 0:160], right, ((1,), (0,)))
+        picked = jnp.concatenate([picked[0:160] + rest, picked[160:]], axis=0)
         rows = [
             jnp.sum(picked[c * 32 : c * 32 + 32] * mask, axis=0, keepdims=True) for c in range(9)
         ]
@@ -450,13 +451,15 @@
             [feat_in[pl.ds(base, LINE)].reshape(LINE * 8, LANES) for base in bases], axis=0
         )
         count = arrived.shape[0]
-        stack = jnp.concatenate(pieces(arrived, 3), axis=0)
+        three = pieces(arrived, 3)
+        stacks = [jnp.concatenate(three, axis=0), jnp.concatenate(three[0:2], axis=0)]
         for at in range(ROWS // 256):
             lanes = slice(at * 256, at * 256 + 256)
             owners_here = owner_row[:, lanes]
             for side, hot in enumerate((place_left, place_right)):
-                found = dot(stack, hot[:, lanes], ((1,), (0,)))
-                found = found[0:count] + found[count : 2 * count] + found[2 * count :]
+                found = dot(stacks[side], hot[:, lanes], ((1,), (0,)))
+                summed_pieces = found[0:count] + found[count : 2 * count]
+                found = summed_pieces + found[2 * count :] if side == 0 else summed_pieces
                 total = halves[side][at]
                 for n, base in enumerate(bases):
                     for step in range(LINE):
@@ -748,8 +751,8 @@
     image, grads = pl.pallas_call(
         functools.partial(kernel, owners, views),
         out_shape=(
-            jax.ShapeDtypeStruct((6 * TILES, LANES), F32),
-            jax.ShapeDtypeStruct((count, owned // views), F32),
+            vmem((6 * TILES, LANES), F32),
+            vmem((count, owned // views), F32),
         ),
         in_specs=[anywhere] * 6,
         out_specs=(anywhere, anywhere),

time: 45.8 us -> 43.3 us (0.945)
  local copies, waits for them, and re-layouts: 3.09 us -> 1.32 us
  Pallas kernels: 41.8 us -> 41.2 us
    unnamed x2, local copies, waits for them, and re-layouts: 3.09 us -> 1.32 us
    pallas_call x1, Pallas kernels: 41.8 us -> 41.2 us  [local(): pl.pallas_call(functools.partial(kernel, owners, views), out_shape=(vmem(...]
where the time goes in v2:
time: 43.3 us; the launch traced here: 43.1 us
  Pallas kernels  41.2 us (95%)
  local copies, waits for them, and re-layouts  1.32 us (3%)
  between operations  0.64 us (1%)
    pallas_call x1, Pallas kernels, local(): pl.pallas_call(functools.partial(kernel, owners, views), out_shape=(vmem(...  41.2 us
    unnamed x2, local copies, waits for them, and re-layouts  1.32 us

profile of v2, /device:TPU:1, one launch (start us, length us, event | category | flops | bytes accessed | tf_op | source)
XLA Modules:
  0.0 43.1 jit_solution(1738101005508114146)
XLA Ops:
  0.6 41.2 %shard_map.77 = (f32[96,128]{1,0:T(8,128)S(1)}, f32[59,1024]{1,0:T(8,128)S(1)}) custom-call(f32[59,8192]{1,0:T(8,128)} %params_ref.1, f32[1,3]{1,0:T(1,128)} %cam_ref.1, s32[1,1,32,64]{3,2,1,0:T(8,128)} %ids_ref.1, s32[1,16,64]{2,1,0:T(8,128)} %slots_ref.1, s32[1,16]{1,0:T(1,128)} %len_ref.1, f32[96,128]{1,0:T(8,128)} %bitcast.3), custom_call_target="tpu_custom_call" | custom-call | flops 2000000000 | bytes 4000000 | tf_op jit(solution)/shard_map/pallas_call | solution.py:751
  41.8 0.6 %copy.12 = f32[1,3,4096]{2,0,1:T(1,128)} copy(f32[1,3,4096]{2,0,1:T(1,128)S(1)} %bitcast.2) | data formatting | bytes 98304
  42.4 0.7 %copy.13 = f32[59,1024]{1,0:T(8,128)} copy(f32[59,1024]{1,0:T(8,128)S(1)} %get-tuple-element.11) | data formatting | bytes 483328

commit v3 on v2

--- a/solution.py
+++ b/solution.py
@@ -353,16 +353,19 @@
         lanes = pl.ds(pl.multiple_of(half * LANES, LANES), LANES)
         for c in range(9):
             for s, piece in enumerate(pieces(values[c], 3)):
-                table[s, pl.ds(pl.multiple_of(c * 32 + inner * 16, 16), 16), lanes] = piece
+                if s < 2 or c < 5:
+                    row = s * 288 + c * 32 + inner * 16
+                    table[pl.ds(pl.multiple_of(row, 16), 16), lanes] = piece
         return carry
 
     lax.fori_loop(0, blocks // 16, features_body, 0)
 
     lane_half = iota((8, LANES), 1) < CAP
 
-    def serve(i, first):
-        for peer in peers(i, first):
-            ids_copy(peer, peer).wait_recv()
+    rings = [[i for i in range(planes) if (i + 1) // 2 <= 1]]
+    rings += [[i for i in range(planes) if (i + 1) // 2 == far] for far in range(2, planes // 2 + 1)]
+
+    def serve(i):
         base = plane(i) * LINE
         ids = jnp.concatenate(
             [ids_in[base] + ids_in[base + 1], ids_in[base + 2] + ids_in[base + 3]], axis=1
@@ -374,10 +377,9 @@
         low_hot[:, lanes] = right
         mask = (iota((32, LINE * CAP), 0) == high).astype(F32)
         high_hot[:, lanes] = mask.astype(BF16)
-        picked = dot(table[0], right, ((1,), (0,)))
-        picked += dot(table[1], right, ((1,), (0,)))
-        rest = dot(table[2, 0:160], right, ((1,), (0,)))
-        picked = jnp.concatenate([picked[0:160] + rest, picked[160:]], axis=0)
+        short = dot(table[0:288], right, ((1,), (0,))) + dot(table[288:576], right, ((1,), (0,)))
+        rest = dot(table[576:736], right, ((1,), (0,)))
+        picked = jnp.concatenate([short[0:160] + rest, short[160:]], axis=0)
         rows = [
             jnp.sum(picked[c * 32 : c * 32 + 32] * mask, axis=0, keepdims=True) for c in range(9)
         ]
@@ -389,15 +391,16 @@
             b = right_group[:, part * LANES : (part + 1) * LANES]
             feat_out[base + 2 * part] = jnp.where(lane_half, a, pltpu.roll(b, CAP, 1))
             feat_out[base + 2 * part + 1] = jnp.where(lane_half, pltpu.roll(a, CAP, 1), b)
-        for peer in peers(i, first):
-            feat_copy(peer, me).start()
-
-    def serve_body(i, carry):
-        serve(i, False)
-        return carry
-
-    serve(0, True)
-    lax.fori_loop(1, planes, serve_body, 0)
+
+    for ring in rings:
+        for i in ring:
+            for peer in peers(i, i == 0):
+                ids_copy(peer, peer).wait_recv()
+        for i in ring:
+            serve(i)
+        for i in ring[::-1]:
+            for peer in peers(i, i == 0):
+                feat_copy(peer, me).start()
     feat_in[me] = feat_out[me]
 
     slots_load.wait()
@@ -520,7 +523,7 @@
         split_b[rows, :] = low
         return through - blend
 
-    lax.fori_loop(0, ENTRIES, forward_body, jnp.ones((TILES, PIXELS), F32))
+    lax.fori_loop(0, ENTRIES, forward_body, jnp.ones((TILES, PIXELS), F32), unroll=8)
 
     def backward_body(step, behind):
         rows = pl.ds(pl.multiple_of((ENTRIES - 1 - step) * TILES, TILES), TILES)
@@ -530,7 +533,7 @@
         split_d[rows, :] = low
         return behind + alpha_all[rows, :] * gain
 
-    lax.fori_loop(0, ENTRIES, backward_body, jnp.zeros((TILES, PIXELS), F32))
+    lax.fori_loop(0, ENTRIES, backward_body, jnp.zeros((TILES, PIXELS), F32), unroll=8)
 
     moments = dot(monomials_two, split_c[...], ((1,), (1,))) + dot(
         monomials_two, split_d[...], ((1,), (1,))
@@ -598,9 +601,8 @@
             for peer in peers(i, i == 0):
                 grad_copy(peer, me).start()
 
-    order = list(range(planes))[::-1]
-    for at in range(0, planes, 2):
-        give(order[at : at + 2])
+    for ring in rings[::-1]:
+        give(ring[::-1])
     grad_in[me] = grad_out[me]
 
     color_both = jnp.concatenate([color_high, color_low], axis=0)
@@ -617,39 +619,42 @@
     wait_sent(ids_copy)
     wait_sent(feat_copy)
 
-    def scatter(i, first):
-        for peer in peers(i, first):
-            grad_copy(peer, peer).wait_recv()
-        base = plane(i) * LINE
-        lanes = pl.ds(pl.multiple_of(base * CAP, LINE * CAP), LINE * CAP)
-        tops = []
-        bottoms = []
-        for part in range(2):
-            even = grad_in[base + 2 * part]
-            odd = grad_in[base + 2 * part + 1]
-            tops.append(jnp.where(lane_half, even, pltpu.roll(odd, CAP, 1)))
-            bottoms.append(jnp.where(lane_half, pltpu.roll(even, CAP, 1), odd))
-        a = jnp.concatenate(tops, axis=1)
-        b = jnp.concatenate(bottoms, axis=1)
-        mask = high_hot[:, lanes]
-        for c in range(9):
-            row = a[c : c + 1] if c < 5 else b[c - 5 : c - 4]
-            for s, piece in enumerate(pieces(jnp.broadcast_to(row, (32, LINE * CAP)), 2)):
-                wide[s * 288 + c * 32 : s * 288 + c * 32 + 32, :] = piece * mask
-        placed = dot(wide[...], low_hot[:, lanes], ((1,), (1,)))
-        placed = placed[0:288] + placed[288:576]
-        if first:
-            gathered[...] = placed
+    def scatter(ring):
+        for i in ring:
+            for peer in peers(i, i == 0):
+                grad_copy(peer, peer).wait_recv()
+        hots = []
+        for n, i in enumerate(ring):
+            base = plane(i) * LINE
+            lanes = pl.ds(pl.multiple_of(base * CAP, LINE * CAP), LINE * CAP)
+            tops = []
+            bottoms = []
+            for part in range(2):
+                even = grad_in[base + 2 * part]
+                odd = grad_in[base + 2 * part + 1]
+                tops.append(jnp.where(lane_half, even, pltpu.roll(odd, CAP, 1)))
+                bottoms.append(jnp.where(lane_half, pltpu.roll(even, CAP, 1), odd))
+            a = jnp.concatenate(tops, axis=1)
+            b = jnp.concatenate(bottoms, axis=1)
+            mask = high_hot[:, lanes]
+            into = slice(n * LINE * CAP, (n + 1) * LINE * CAP)
+            for c in range(9):
+                row = a[c : c + 1] if c < 5 else b[c - 5 : c - 4]
+                for s, piece in enumerate(pieces(jnp.broadcast_to(row, (32, LINE * CAP)), 2)):
+                    wide[s * 288 + c * 32 : s * 288 + c * 32 + 32, into] = piece * mask
+            hots.append(low_hot[:, lanes])
+        placed = dot(wide[:, 0 : len(ring) * LINE * CAP], jnp.concatenate(hots, axis=1), ((1,), (1,)))
+        return placed[0:288] + placed[288:576]
+
+    for ring in rings[:-1]:
+        if ring[0] == 0:
+            gathered[...] = scatter(ring)
         else:
-            gathered[...] += placed
-
-    def scatter_body(i, carry):
-        scatter(i, False)
-        return carry
-
-    scatter(0, True)
-    lax.fori_loop(1, planes, scatter_body, 0)
-    placed = gathered[...].reshape(9, 32, 256)
+            gathered[...] += scatter(ring)
+    placed = scatter(rings[-1])
+    if len(rings) > 1:
+        placed = placed + gathered[...]
+    placed = placed.reshape(9, 32, 256)
     dense[:, 0:32, :] = placed[:, :, 0:LANES]
     dense[:, 32:64, :] = placed[:, :, LANES:256]
 
@@ -769,12 +774,12 @@
             vmem((owners, 1, LANES), jnp.int32),
             vmem((8, LANES), F32),
             vmem((views, 8, LANES), F32),
-            vmem((3, 288, 256), BF16),
+            vmem((736, 256), BF16),
             vmem((256, slots_all), BF16),
             vmem((32, slots_all), BF16),
             vmem((owners, 8, LANES), F32),
             vmem((owners, 8, LANES), F32),
-            vmem((576, LINE * CAP), BF16),
+            vmem((576, 3 * LINE * CAP), BF16),
             vmem((288, 256), F32),
             vmem((ROWS, PIXELS), F32),
             vmem((ROWS, PIXELS), F32),

time: 43.3 us -> 42.4 us (0.979)
  Pallas kernels: 41.2 us -> 40.3 us
    pallas_call x1, Pallas kernels: 41.2 us -> 40.3 us  [local(): pl.pallas_call(functools.partial(kernel, owners, views), out_shape=(vmem(...]
where the time goes in v3:
time: 42.4 us; the launch traced here: 42.3 us
  Pallas kernels  40.3 us (95%)
  local copies, waits for them, and re-layouts  1.32 us (3%)
  between operations  0.64 us (2%)
    pallas_call x1, Pallas kernels, local(): pl.pallas_call(functools.partial(kernel, owners, views), out_shape=(vmem(...  40.3 us
    unnamed x2, local copies, waits for them, and re-layouts  1.32 us

profile of v3, /device:TPU:1, one launch (start us, length us, event | category | flops | bytes accessed | tf_op | source)
XLA Modules:
  0.0 42.3 jit_solution(4033739078202190807)
XLA Ops:
  0.6 40.3 %shard_map.77 = (f32[96,128]{1,0:T(8,128)S(1)}, f32[59,1024]{1,0:T(8,128)S(1)}) custom-call(f32[59,8192]{1,0:T(8,128)} %params_ref.1, f32[1,3]{1,0:T(1,128)} %cam_ref.1, s32[1,1,32,64]{3,2,1,0:T(8,128)} %ids_ref.1, s32[1,16,64]{2,1,0:T(8,128)} %slots_ref.1, s32[1,16]{1,0:T(1,128)} %len_ref.1, f32[96,128]{1,0:T(8,128)} %bitcast.3), custom_call_target="tpu_custom_call" | custom-call | flops 2000000000 | bytes 4000000 | tf_op jit(solution)/shard_map/pallas_call | solution.py:756
  40.9 0.6 %copy.12 = f32[1,3,4096]{2,0,1:T(1,128)} copy(f32[1,3,4096]{2,0,1:T(1,128)S(1)} %bitcast.2) | data formatting | bytes 98304
  41.6 0.7 %copy.13 = f32[59,1024]{1,0:T(8,128)} copy(f32[59,1024]{1,0:T(8,128)S(1)} %get-tuple-element.11) | data formatting | bytes 483328

commit v4 on v3

--- a/solution.py
+++ b/solution.py
@@ -135,16 +135,14 @@
     slots_ref,
     len_ref,
     cot_ref,
-    image_ref,
-    grads_ref,
+    image,
+    summed,
     held,
     asked,
     cam_held,
     slots_held,
     len_held,
     held_cot,
-    image,
-    summed,
     ids_out,
     ids_in,
     cam_out,
@@ -169,7 +167,6 @@
     dense,
     view_in,
     load_sem,
-    store_sem,
     ids_s,
     ids_r,
     feat_s,
@@ -523,7 +520,15 @@
         split_b[rows, :] = low
         return through - blend
 
-    lax.fori_loop(0, ENTRIES, forward_body, jnp.ones((TILES, PIXELS), F32), unroll=8)
+    lax.fori_loop(0, ENTRIES, forward_body, jnp.ones((TILES, PIXELS), F32), unroll=True)
+
+    cot_both = jnp.concatenate([cot_high, cot_low], axis=0)
+    by_color = dot(cot_both, split_a[...], ((1,), (1,)))
+    by_color = (
+        by_color[0 : 3 * TILES]
+        + by_color[3 * TILES :]
+        + dot(cot_high, split_b[...], ((1,), (1,)))
+    )
 
     def backward_body(step, behind):
         rows = pl.ds(pl.multiple_of((ENTRIES - 1 - step) * TILES, TILES), TILES)
@@ -533,17 +538,10 @@
         split_d[rows, :] = low
         return behind + alpha_all[rows, :] * gain
 
-    lax.fori_loop(0, ENTRIES, backward_body, jnp.zeros((TILES, PIXELS), F32), unroll=8)
+    lax.fori_loop(0, ENTRIES, backward_body, jnp.zeros((TILES, PIXELS), F32), unroll=True)
 
     moments = dot(monomials_two, split_c[...], ((1,), (1,))) + dot(
         monomials_two, split_d[...], ((1,), (1,))
-    )
-    cot_both = jnp.concatenate([cot_high, cot_low], axis=0)
-    by_color = dot(cot_both, split_a[...], ((1,), (1,)))
-    by_color = (
-        by_color[0 : 3 * TILES]
-        + by_color[3 * TILES :]
-        + dot(cot_high, split_b[...], ((1,), (1,)))
     )
     grad_colors = [
         jnp.sum(by_color[c * TILES : (c + 1) * TILES] * tile_mask, axis=0, keepdims=True)
@@ -614,7 +612,6 @@
     )
     for half in range(2):
         image[pl.ds(half, 3 * TILES, stride=2), :] = shown[:, half * LANES : half * LANES + LANES]
-    pltpu.make_async_copy(image, image_ref, store_sem.at[0]).start()
 
     wait_sent(ids_copy)
     wait_sent(feat_copy)
@@ -674,7 +671,6 @@
 
     lax.fori_loop(1, views, cam_wait, 0)
     wait_sent(grad_copy)
-    pltpu.make_async_copy(image, image_ref, store_sem.at[0]).wait()
 
     def get(r):
         return held[r, mine, :]
@@ -724,25 +720,22 @@
         summed[3 + r] = by_shape[r]
     summed[10] = totals[3] / (1.0 + jnp.exp(get(10)))
 
-    def store_grads(j):
-        return pltpu.make_async_copy(
-            summed.at[:, j, :],
-            grads_ref.at[:, pl.ds(pl.multiple_of(j * LANES, LANES), LANES)],
-            store_sem.at[1],
-        )
-
-    def store_grads_body(j, carry):
-        store_grads(j).start()
-        return carry
-
-    lax.fori_loop(0, chunk, store_grads_body, 0)
-
     def view_wait(off, carry):
         view_copy(lax.rem(my_view + off, views), my_view).wait_send()
         return carry
 
     lax.fori_loop(1, views, view_wait, 0)
-    pltpu.make_async_copy(summed, summed, store_sem.at[1]).wait()
+
+
+def store_kernel(image, summed, image_ref, grads_ref, sems):
+    image_store = pltpu.make_async_copy(image, image_ref, sems.at[0])
+    image_store.start()
+    for j in range(summed.shape[1]):
+        pltpu.make_async_copy(
+            summed.at[:, j, :], grads_ref.at[:, j * LANES : (j + 1) * LANES], sems.at[1]
+        ).start()
+    image_store.wait()
+    pltpu.make_async_copy(summed, summed, sems.at[1]).wait()
 
 
 def local(owners, views, params, cam_pos, req_ids, tile_slots, tile_len, cotangent):
@@ -753,14 +746,15 @@
     vmem = pltpu.VMEM
     dma = pltpu.SemaphoreType.DMA
     anywhere = pl.BlockSpec(memory_space=pl.ANY)
-    image, grads = pl.pallas_call(
+    inside = pl.BlockSpec(memory_space=vmem)
+    image, summed = pl.pallas_call(
         functools.partial(kernel, owners, views),
         out_shape=(
             vmem((6 * TILES, LANES), F32),
-            vmem((count, owned // views), F32),
+            vmem((count, chunk, LANES), F32),
         ),
         in_specs=[anywhere] * 6,
-        out_specs=(anywhere, anywhere),
+        out_specs=(inside, inside),
         scratch_shapes=[
             vmem((count, blocks, LANES), F32),
             vmem((owners, CAP), jnp.int32),
@@ -768,8 +762,6 @@
             vmem((TILES, ENTRIES), jnp.int32),
             vmem((1, TILES), jnp.int32),
             vmem((6 * TILES, LANES), F32),
-            vmem((6 * TILES, LANES), F32),
-            vmem((count, chunk, LANES), F32),
             vmem((owners, 1, LANES), jnp.int32),
             vmem((owners, 1, LANES), jnp.int32),
             vmem((8, LANES), F32),
@@ -794,7 +786,6 @@
             vmem((9, blocks, LANES), F32),
             vmem((views, 9, chunk, LANES), F32),
             dma((6,)),
-            dma((2,)),
         ]
         + [dma((owners,)) for _ in range(6)]
         + [dma((views,)) for _ in range(4)],
@@ -812,6 +803,16 @@
         tile_len,
         cotangent.reshape(6 * TILES, LANES),
     )
+    image, grads = pl.pallas_call(
+        store_kernel,
+        out_shape=(
+            pltpu.HBM((6 * TILES, LANES), F32),
+            pltpu.HBM((count, owned // views), F32),
+        ),
+        in_specs=[inside] * 2,
+        out_specs=(anywhere, anywhere),
+        scratch_shapes=[dma((2,))],
+    )(image, summed)
     return image.reshape(cotangent.shape), grads
 
 

time: 42.4 us -> 43 us (1.014)
  Pallas kernels: 40.3 us -> 40.9 us
    pallas_call x0 -> x1, Pallas kernels: none -> 1.7 us  [local(): pl.pallas_call(store_kernel, out_shape=(pltpu.HBM((6 * TILES, LANES), F32...]
    pallas_call x1, Pallas kernels: 40.3 us -> 39.2 us  [local(): pl.pallas_call(functools.partial(kernel, owners, views), out_shape=(vmem(...]
    unnamed x2 -> x4, local copies, waits for them, and re-layouts: 1.32 us -> 1.3 us
where the time goes in v4:
time: 43 us; the launch traced here: 42.8 us
  Pallas kernels  40.9 us (95%)
  local copies, waits for them, and re-layouts  1.3 us (3%)
  between operations  0.65 us (2%)
    pallas_call x1, Pallas kernels, local(): pl.pallas_call(functools.partial(kernel, owners, views), out_shape=(vmem(...  39.2 us
    pallas_call x1, Pallas kernels, local(): pl.pallas_call(store_kernel, out_shape=(pltpu.HBM((6 * TILES, LANES), F32...  1.7 us
    unnamed x4, local copies, waits for them, and re-layouts  1.3 us

profile of v4, /device:TPU:1, one launch (start us, length us, event | category | flops | bytes accessed | tf_op | source)
XLA Modules:
  0.0 42.8 jit_solution(2818505524869385883)
XLA Ops:
  0.6 39.2 %shard_map.77 = (f32[96,128]{1,0:T(8,128)S(1)}, f32[59,8,128]{2,1,0:T(8,128)S(1)}) custom-call(f32[59,8192]{1,0:T(8,128)} %params_ref.1, f32[1,3]{1,0:T(1,128)} %cam_ref.1, s32[1,1,32,64]{3,2,1,0:T(8,128)} %ids_ref.1, s32[1,16,64]{2,1,0:T(8,128)} %slots_ref.1, s32[1,16]{1,0:T(1,128)} %len_ref.1, f32[96,128]{1,0:T(8,128)} %bitcast.2), custom_call_target="tpu_custom_call" | custom-call | flops 2000000000 | bytes 4000000 | tf_op jit(solution)/shard_map/pallas_call | solution.py:750
  39.8 0.0 copy-start
  39.8 0.7 %copy-done = f32[59,8,128]{2,1,0:T(8,128)} copy-done((f32[59,8,128]{2,1,0:T(8,128)}, f32[59,8,128]{2,1,0:T(8,128)S(1)}, u32[]{:S(2)}) %copy-start) | copy-done | bytes 241688
  40.5 0.0 copy-start.1
  40.5 0.6 %copy-done.1 = f32[96,128]{1,0:T(8,128)} copy-done((f32[96,128]{1,0:T(8,128)}, f32[96,128]{1,0:T(8,128)S(1)}, u32[]{:S(2)}) %copy-start.1) | copy-done | bytes 49176
  41.1 1.7 %shard_map.78 = (f32[96,128]{1,0:T(8,128)}, f32[59,1024]{1,0:T(8,128)}) custom-call(f32[96,128]{1,0:T(8,128)} %copy-done.1, f32[59,8,128]{2,1,0:T(8,128)} %copy-done), custom_call_target="tpu_custom_call" | custom-call | tf_op jit(solution)/shard_map/pallas_call | solution.py:806
Async XLA Ops:
  39.8 0.7 %copy-start = (f32[59,8,128]{2,1,0:T(8,128)}, f32[59,8,128]{2,1,0:T(8,128)S(1)}, u32[]{:S(2)}) copy-start(f32[59,8,128]{2,1,0:T(8,128)S(1)} %get-tuple-element.7.summed) | copy-start | bytes 724996
  40.5 0.6 %copy-start.1 = (f32[96,128]{1,0:T(8,128)}, f32[96,128]{1,0:T(8,128)S(1)}, u32[]{:S(2)}) copy-start(f32[96,128]{1,0:T(8,128)S(1)} %get-tuple-element.6.image) | copy-start | bytes 147460

commit v5 on v4

--- a/solution.py
+++ b/solution.py
@@ -812,6 +812,7 @@
         in_specs=[inside] * 2,
         out_specs=(anywhere, anywhere),
         scratch_shapes=[dma((2,))],
+        compiler_params=pltpu.CompilerParams(vmem_limit_bytes=4 * 1024 * 1024),
     )(image, summed)
     return image.reshape(cotangent.shape), grads
 

time: 43 us -> 40.7 us (0.947)
  local copies, waits for them, and re-layouts: 1.3 us -> 0 us
  Pallas kernels: 40.9 us -> 39.9 us
    unnamed x4 -> x0, local copies, waits for them, and re-layouts: 1.3 us -> none
    pallas_call x1, Pallas kernels: 1.7 us -> 0.73 us  [local(): pl.pallas_call(store_kernel, out_shape=(pltpu.HBM((6 * TILES, LANES), F32...]
where the time goes in v5:
time: 40.7 us; the launch traced here: 40.5 us
  Pallas kernels  39.9 us (98%)
  between operations  0.64 us (2%)
    pallas_call x1, Pallas kernels, local(): pl.pallas_call(functools.partial(kernel, owners, views), out_shape=(vmem(...  39.2 us

profile of v5, /device:TPU:1, one launch (start us, length us, event | category | flops | bytes accessed | tf_op | source)
XLA Modules:
  0.0 40.5 jit_solution(12109241498660354060)
XLA Ops:
  0.6 39.2 %shard_map.77 = (f32[96,128]{1,0:T(8,128)S(1)}, f32[59,8,128]{2,1,0:T(8,128)S(1)}) custom-call(f32[59,8192]{1,0:T(8,128)} %params_ref.1, f32[1,3]{1,0:T(1,128)} %cam_ref.1, s32[1,1,32,64]{3,2,1,0:T(8,128)} %ids_ref.1, s32[1,16,64]{2,1,0:T(8,128)} %slots_ref.1, s32[1,16]{1,0:T(1,128)} %len_ref.1, f32[96,128]{1,0:T(8,128)} %bitcast.2), custom_call_target="tpu_custom_call" | custom-call | flops 2000000000 | bytes 4000000 | tf_op jit(solution)/shard_map/pallas_call | solution.py:750
  39.8 0.7 %shard_map.78 = (f32[96,128]{1,0:T(8,128)}, f32[59,1024]{1,0:T(8,128)}) custom-call(f32[96,128]{1,0:T(8,128)S(1)} %get-tuple-element.6.image, f32[59,8,128]{2,1,0:T(8,128)S(1)} %get-tuple-element.7.summed), custom_call_target="tpu_custom_call" | custom-call | tf_op jit(solution)/shard_map/pallas_call | solution.py:806

commit v6 on v5

--- a/solution.py
+++ b/solution.py
@@ -655,11 +655,9 @@
     dense[:, 0:32, :] = placed[:, :, 0:LANES]
     dense[:, 32:64, :] = placed[:, :, LANES:256]
 
-    def view_send(step, carry):
-        view_copy(view_peer(views - 1 - step), my_view).start()
-        return carry
-
-    lax.fori_loop(0, views - 1, view_send, 0)
+    order = [7, 5, 3, 6, 2, 4, 1] if views == 8 else list(range(1, views))[::-1]
+    for i in order:
+        view_copy(view_peer(i), my_view).start()
     mine = pl.ds(pl.multiple_of(my_view * chunk, chunk), chunk)
     view_in[my_view] = dense[:, mine, :]
 
@@ -682,37 +680,52 @@
 
     sigma, shape_back = jax.vjp(shape_of, scale_quat)
     zero = jnp.zeros((chunk, LANES), F32)
-    for r in range(59):
-        summed[r] = zero
-
-    def add_view(v, totals):
-        camera = cam_in[v]
-        x = get(0) - camera[0:1]
-        y = get(1) - camera[1:2]
-        z = get(2) - camera[2:3]
-        grads = [view_in[v, c] for c in range(9)]
-        _, geometry_back = jax.vjp(geometry, x, y, z, sigma)
-        gx, gy, gz, g_sigma = geometry_back(tuple(grads[0:5]))
-        basis, basis_back = jax.vjp(harmonic_basis, x, y, z)
-        g_basis = [zero] * 15
+
+    def add_views(members, totals, first):
+        held_grads = []
+        bases = []
+        backs = []
+        for v in members:
+            camera = cam_in[v]
+            x = get(0) - camera[0:1]
+            y = get(1) - camera[1:2]
+            z = get(2) - camera[2:3]
+            grads = [view_in[v, c] for c in range(9)]
+            _, geometry_back = jax.vjp(geometry, x, y, z, sigma)
+            gx, gy, gz, g_sigma = geometry_back(tuple(grads[0:5]))
+            add = [gx, gy, gz, grads[5]] + list(g_sigma)
+            totals = tuple(t + a for t, a in zip(totals, add))
+            basis, basis_back = jax.vjp(harmonic_basis, x, y, z)
+            held_grads.append(grads[6:9])
+            bases.append(basis)
+            backs.append(basis_back)
+        g_bases = [[zero] * 15 for _ in members]
         for c in range(3):
-            color_grad = grads[6 + c]
-            summed[11 + 16 * c] += sh_zero * color_grad
-            for k in range(15):
-                row = 12 + 16 * c + k
-                summed[row] += basis[k] * color_grad
-                g_basis[k] = g_basis[k] + get(row) * color_grad
-        hx, hy, hz = basis_back(g_basis)
-        add = [gx + hx, gy + hy, gz + hz, grads[5]] + list(g_sigma)
-        return tuple(t + a for t, a in zip(totals, add))
-
-    def view_body(i, totals):
-        peer = view_peer(i)
-        view_copy(peer, peer).wait_recv()
-        return add_view(peer, totals)
-
-    totals = add_view(my_view, tuple([zero] * 10))
-    totals = lax.fori_loop(1, views, view_body, totals)
+            for k in range(16):
+                row = 11 + 16 * c + k
+                total = zero if first else summed[row]
+                for n in range(len(members)):
+                    color_grad = held_grads[n][c]
+                    if k == 0:
+                        total = total + sh_zero * color_grad
+                    else:
+                        total = total + bases[n][k - 1] * color_grad
+                        g_bases[n][k - 1] = g_bases[n][k - 1] + get(row) * color_grad
+                summed[row] = total
+        for n in range(len(members)):
+            by_direction = backs[n](g_bases[n])
+            totals = tuple(t + a for t, a in zip(totals[0:3], by_direction)) + totals[3:]
+        return totals
+
+    totals = tuple([zero] * 10)
+    for at in range(0, views, 2):
+        members = []
+        for i in (at, at + 1):
+            peer = my_view if i == 0 else view_peer(i)
+            if i > 0:
+                view_copy(peer, peer).wait_recv()
+            members.append(peer)
+        totals = add_views(members, totals, at == 0)
     for r in range(3):
         summed[r] = totals[r]
     (by_shape,) = shape_back(list(totals[4:10]))

time: 40.7 us -> 40.1 us (0.985)
  Pallas kernels: 39.9 us -> 39.3 us
    pallas_call x1, Pallas kernels: 39.2 us -> 38.6 us  [local(): pl.pallas_call(functools.partial(kernel, owners, views), out_shape=(vmem(...]
where the time goes in v6:
time: 40.1 us; the launch traced here: 40 us
  Pallas kernels  39.3 us (98%)
  between operations  0.64 us (2%)
    pallas_call x1, Pallas kernels, local(): pl.pallas_call(functools.partial(kernel, owners, views), out_shape=(vmem(...  38.6 us

profile of v6, /device:TPU:1, one launch (start us, length us, event | category | flops | bytes accessed | tf_op | source)
XLA Modules:
  0.0 40.0 jit_solution(12083099714772644115)
XLA Ops:
  0.6 38.6 %shard_map.77 = (f32[96,128]{1,0:T(8,128)S(1)}, f32[59,8,128]{2,1,0:T(8,128)S(1)}) custom-call(f32[59,8192]{1,0:T(8,128)} %params_ref.1, f32[1,3]{1,0:T(1,128)} %cam_ref.1, s32[1,1,32,64]{3,2,1,0:T(8,128)} %ids_ref.1, s32[1,16,64]{2,1,0:T(8,128)} %slots_ref.1, s32[1,16]{1,0:T(1,128)} %len_ref.1, f32[96,128]{1,0:T(8,128)} %bitcast.2), custom_call_target="tpu_custom_call" | custom-call | flops 2000000000 | bytes 4000000 | tf_op jit(solution)/shard_map/pallas_call | solution.py:763
  39.2 0.7 %shard_map.78 = (f32[96,128]{1,0:T(8,128)}, f32[59,1024]{1,0:T(8,128)}) custom-call(f32[96,128]{1,0:T(8,128)S(1)} %get-tuple-element.6.image, f32[59,8,128]{2,1,0:T(8,128)S(1)} %get-tuple-element.7.summed), custom_call_target="tpu_custom_call" | custom-call | tf_op jit(solution)/shard_map/pallas_call | solution.py:819

commit v7 on v6

--- a/solution.py
+++ b/solution.py
@@ -310,14 +310,9 @@
 
     pl.semaphore_wait(barrier, owners + views - 2)
 
-    def ids_body(step, carry):
-        for peer in peers(planes - 1 - step, False):
+    for i in [planes - 1] + list(range(planes - 1)):
+        for peer in peers(i, i == 0):
             ids_copy(peer, me).start()
-        return carry
-
-    lax.fori_loop(0, planes - 1, ids_body, 0)
-    for peer in peers(0, True):
-        ids_copy(peer, me).start()
 
     def cam_send(off, carry):
         cam_copy(lax.rem(my_view + off, views), my_view).start()
@@ -361,6 +356,8 @@
 
     rings = [[i for i in range(planes) if (i + 1) // 2 <= 1]]
     rings += [[i for i in range(planes) if (i + 1) // 2 == far] for far in range(2, planes // 2 + 1)]
+
+    joined = rings[:-2] + [rings[-2] + rings[-1]] if len(rings) > 2 else rings
 
     def serve(i):
         base = plane(i) * LINE
@@ -389,7 +386,7 @@
             feat_out[base + 2 * part] = jnp.where(lane_half, a, pltpu.roll(b, CAP, 1))
             feat_out[base + 2 * part + 1] = jnp.where(lane_half, pltpu.roll(a, CAP, 1), b)
 
-    for ring in rings:
+    for ring in joined:
         for i in ring:
             for peer in peers(i, i == 0):
                 ids_copy(peer, peer).wait_recv()

time: 40.1 us -> 39.8 us (level)
  no operation moved by 1% of the time
where the time goes in v7:
time: 39.8 us; the launch traced here: 39.6 us
  Pallas kernels  39 us (98%)
  between operations  0.64 us (2%)
    pallas_call x1, Pallas kernels, local(): pl.pallas_call(functools.partial(kernel, owners, views), out_shape=(vmem(...  38.2 us

profile of v7, /device:TPU:1, one launch (start us, length us, event | category | flops | bytes accessed | tf_op | source)
XLA Modules:
  0.0 39.6 jit_solution(16629624415103456096)
XLA Ops:
  0.6 38.2 %shard_map.77 = (f32[96,128]{1,0:T(8,128)S(1)}, f32[59,8,128]{2,1,0:T(8,128)S(1)}) custom-call(f32[59,8192]{1,0:T(8,128)} %params_ref.1, f32[1,3]{1,0:T(1,128)} %cam_ref.1, s32[1,1,32,64]{3,2,1,0:T(8,128)} %ids_ref.1, s32[1,16,64]{2,1,0:T(8,128)} %slots_ref.1, s32[1,16]{1,0:T(1,128)} %len_ref.1, f32[96,128]{1,0:T(8,128)} %bitcast.2), custom_call_target="tpu_custom_call" | custom-call | flops 2000000000 | bytes 4000000 | tf_op jit(solution)/shard_map/pallas_call | solution.py:760
  38.9 0.7 %shard_map.78 = (f32[96,128]{1,0:T(8,128)}, f32[59,1024]{1,0:T(8,128)}) custom-call(f32[96,128]{1,0:T(8,128)S(1)} %get-tuple-element.6.image, f32[59,8,128]{2,1,0:T(8,128)S(1)} %get-tuple-element.7.summed), custom_call_target="tpu_custom_call" | custom-call | tf_op jit(solution)/shard_map/pallas_call | solution.py:816

commit v8 on v7

--- a/solution.py
+++ b/solution.py
@@ -194,7 +194,8 @@
         return lax.rem(my_z + odd * half + (1 - odd) * (planes - half), planes)
 
     def peers(i, first):
-        return [plane(i) * LINE + lax.rem(my_y + step, LINE) for step in range(1 if first else 0, LINE)]
+        steps = (2, 1, 3) if first else (2, 1, 3, 0)
+        return [plane(i) * LINE + lax.rem(my_y + step, LINE) for step in steps]
 
     def view_peer(i):
         pair = i // 2

time: 39.8 us -> 39.5 us (level)
  no operation moved by 1% of the time
where the time goes in v8:
time: 39.5 us; the launch traced here: 39.4 us
  Pallas kernels  38.7 us (98%)
  between operations  0.64 us (2%)
    pallas_call x1, Pallas kernels, local(): pl.pallas_call(functools.partial(kernel, owners, views), out_shape=(vmem(...  38 us

profile of v8, /device:TPU:1, one launch (start us, length us, event | category | flops | bytes accessed | tf_op | source)
XLA Modules:
  0.0 39.4 jit_solution(1278203732113530069)
XLA Ops:
  0.6 38.0 %shard_map.77 = (f32[96,128]{1,0:T(8,128)S(1)}, f32[59,8,128]{2,1,0:T(8,128)S(1)}) custom-call(f32[59,8192]{1,0:T(8,128)} %params_ref.1, f32[1,3]{1,0:T(1,128)} %cam_ref.1, s32[1,1,32,64]{3,2,1,0:T(8,128)} %ids_ref.1, s32[1,16,64]{2,1,0:T(8,128)} %slots_ref.1, s32[1,16]{1,0:T(1,128)} %len_ref.1, f32[96,128]{1,0:T(8,128)} %bitcast.2), custom_call_target="tpu_custom_call" | custom-call | flops 2000000000 | bytes 4000000 | tf_op jit(solution)/shard_map/pallas_call | solution.py:761
  38.6 0.7 %shard_map.78 = (f32[96,128]{1,0:T(8,128)}, f32[59,1024]{1,0:T(8,128)}) custom-call(f32[96,128]{1,0:T(8,128)S(1)} %get-tuple-element.6.image, f32[59,8,128]{2,1,0:T(8,128)S(1)} %get-tuple-element.7.summed), custom_call_target="tpu_custom_call" | custom-call | tf_op jit(solution)/shard_map/pallas_call | solution.py:817

commit v9 on v8

--- a/solution.py
+++ b/solution.py
@@ -597,19 +597,10 @@
             for peer in peers(i, i == 0):
                 grad_copy(peer, me).start()
 
-    for ring in rings[::-1]:
+    middle = [i for ring in rings[1:-1] for i in ring]
+    for ring in [rings[0], middle, rings[-1]][::-1] if middle else rings[::-1]:
         give(ring[::-1])
     grad_in[me] = grad_out[me]
-
-    color_both = jnp.concatenate([color_high, color_low], axis=0)
-    shown = dot(color_both, split_a[...], ((1,), (0,)))
-    shown = (
-        shown[0 : 3 * TILES]
-        + shown[3 * TILES :]
-        + dot(color_high, split_b[...], ((1,), (0,)))
-    )
-    for half in range(2):
-        image[pl.ds(half, 3 * TILES, stride=2), :] = shown[:, half * LANES : half * LANES + LANES]
 
     wait_sent(ids_copy)
     wait_sent(feat_copy)
@@ -667,6 +658,16 @@
 
     lax.fori_loop(1, views, cam_wait, 0)
     wait_sent(grad_copy)
+
+    color_both = jnp.concatenate([color_high, color_low], axis=0)
+    shown = dot(color_both, split_a[...], ((1,), (0,)))
+    shown = (
+        shown[0 : 3 * TILES]
+        + shown[3 * TILES :]
+        + dot(color_high, split_b[...], ((1,), (0,)))
+    )
+    for half in range(2):
+        image[pl.ds(half, 3 * TILES, stride=2), :] = shown[:, half * LANES : half * LANES + LANES]
 
     def get(r):
         return held[r, mine, :]

time: 39.5 us -> 39.6 us (level)
  no operation moved by 1% of the time
where the time goes in v9:
time: 39.6 us; the launch traced here: 39.4 us
  Pallas kernels  38.8 us (98%)
  between operations  0.64 us (2%)
    pallas_call x1, Pallas kernels, local(): pl.pallas_call(functools.partial(kernel, owners, views), out_shape=(vmem(...  38 us

profile of v9, /device:TPU:1, one launch (start us, length us, event | category | flops | bytes accessed | tf_op | source)
XLA Modules:
  0.0 39.4 jit_solution(11315195141826201732)
XLA Ops:
  0.6 38.0 %shard_map.77 = (f32[96,128]{1,0:T(8,128)S(1)}, f32[59,8,128]{2,1,0:T(8,128)S(1)}) custom-call(f32[59,8192]{1,0:T(8,128)} %params_ref.1, f32[1,3]{1,0:T(1,128)} %cam_ref.1, s32[1,1,32,64]{3,2,1,0:T(8,128)} %ids_ref.1, s32[1,16,64]{2,1,0:T(8,128)} %slots_ref.1, s32[1,16]{1,0:T(1,128)} %len_ref.1, f32[96,128]{1,0:T(8,128)} %bitcast.2), custom_call_target="tpu_custom_call" | custom-call | flops 2000000000 | bytes 4000000 | tf_op jit(solution)/shard_map/pallas_call | solution.py:762
  38.7 0.7 %shard_map.78 = (f32[96,128]{1,0:T(8,128)}, f32[59,1024]{1,0:T(8,128)}) custom-call(f32[96,128]{1,0:T(8,128)S(1)} %get-tuple-element.6.image, f32[59,8,128]{2,1,0:T(8,128)S(1)} %get-tuple-element.7.summed), custom_call_target="tpu_custom_call" | custom-call | tf_op jit(solution)/shard_map/pallas_call | solution.py:818
